TPU v7x, 32 devices: a whole 2x2x4 slice. The times are simulated.
32 devices in a mesh: tm: 8 (over z, core), fsdp: 4 (over y, x).
Axes of the slice: x: 2, y: 2, z: 4, core: 2. Of those that a mesh axis runs over, the one named last changes fastest.
Arguments:
- queries: bfloat16 [4, 1024, 768], P('fsdp', 'tm'), may hold values from -135 to 135, as said below
- keys_values: bfloat16 [4, 1024, 1536], P('fsdp', 'tm'), may hold values from -4.5 to 4.5
- inputs: bfloat16 [4, 1024, 1536], P('fsdp', 'tm'), may hold values from -6 to 6
- cotangent: bfloat16 [4, 1024, 1536], P('fsdp', 'tm'), may hold values from -6 to 6
- out_weight: bfloat16 [768, 1536], P('fsdp'), may hold values from -0.21875 to 0.21875
- conv_kernel: bfloat16 [32, 1536], P(None, 'fsdp'), may hold values from -1 to 1
- utt_starts: int32 [4, 16], P('fsdp'), may hold values from 0 to 1023, as said below
Outputs:
- context_grad: bfloat16 [4, 1024, 768], P('fsdp', 'tm')
- weight_grad: float32 [768, 1536], P('fsdp')
- kernel_grad: float32 [32, 1536], P(None, 'fsdp')
Inputs may be any that keep to these rules, and one draw needn't show every extreme that they name: In the hidden draw some frames' queries are large multiples of their own keys, so that a few scores are far above the rest. `utt_starts`: each row begins with 0 and rises strictly; entry u is the first frame of utterance u of that packed sequence.
All inputs are finite; a program needn't handle non-finite values.
Results may differ from a plain program's by a relative error of at most 0.014.
Values may be sent and summed in bfloat16 or wider, within the bound.
A program may use at most 128 MiB of HBM per device.

v0:
```python
import math

import jax
import jax.numpy as jnp
from jax import lax
from jax.sharding import PartitionSpec as P

HEADS_W = 8
KW = 32
WIN = 128


masked_score = -1e30


def with_halo(x, sides, width):
    for axis, dim in sides:
        devices, length = (lax.axis_size(axis), x.shape[dim])
        up = [(i, (i + 1) % devices) for i in range(devices - 1)]
        down = [(j, i) for i, j in up]
        last = lax.slice_in_dim(x, length - width, length, axis=dim)
        initial = lax.slice_in_dim(x, 0, width, axis=dim)
        before = lax.ppermute(last, axis, up)
        after = lax.ppermute(initial, axis, down)
        x = jnp.concatenate([before, x, after], axis=dim)
    return x


def segment_ids(starts_row, positions):
    return jnp.sum((starts_row[None, :] <= positions[:, None]).astype(jnp.int32), axis=1) - 1


def shards(queries, keys_values, inputs, cotangent, out_weight, conv_kernel, utt_starts):
    query_rows = queries[0]
    kv_rows = keys_values[0]
    input_rows = inputs[0]
    cotangent_rows = cotangent[0]
    starts_row = utt_starts[0]
    local_frames = query_rows.shape[0]
    head_width = query_rows.shape[1]
    head_size = head_width // HEADS_W
    window_half = WIN // 2
    conv_reach = KW - 1
    conv_lead = KW // 2
    conv_span = local_frames + KW - 1
    frames_total = local_frames * lax.axis_size("tm")
    first_frame = lax.axis_index("tm") * local_frames
    full_weight, full_kernel = (
        lax.all_gather(out_weight, "fsdp", axis=0, tiled=True),
        lax.all_gather(conv_kernel, "fsdp", axis=1, tiled=True),
    )
    kv_ext = with_halo(kv_rows, (("tm", 0),), window_half)
    key_span = local_frames + 2 * window_half
    key_positions = first_frame - window_half + jnp.arange(key_span, dtype=jnp.int32)
    key_seg = jnp.where(key_positions < frames_total, segment_ids(starts_row, key_positions), -1)
    query_seg = segment_ids(starts_row, first_frame + jnp.arange(local_frames, dtype=jnp.int32))
    key_offset = (
        jnp.arange(key_span, dtype=jnp.int32)[None, :]
        - jnp.arange(local_frames, dtype=jnp.int32)[:, None]
    )
    allowed = (
        (key_offset >= 0)
        & (key_offset <= 2 * window_half)
        & (query_seg[:, None] == key_seg[None, :])
    )
    query_heads = query_rows.reshape(local_frames, HEADS_W, head_size)
    key_heads = kv_ext[:, :head_width].reshape(key_span, HEADS_W, head_size)
    value_heads = kv_ext[:, head_width:].reshape(key_span, HEADS_W, head_size)
    scores = jnp.einsum(
        "qhe,khe->hqk", query_heads, key_heads, preferred_element_type=jnp.float32
    ) / math.sqrt(head_size)
    scores = jnp.where(allowed[None], scores, masked_score)
    row_max = jnp.max(scores, axis=2, keepdims=True)
    exp_scores = jnp.exp(scores - row_max)
    attn_probs = (exp_scores / jnp.sum(exp_scores, axis=2, keepdims=True)).astype(jnp.bfloat16)
    context = jnp.einsum(
        "hqk,khe->qhe", attn_probs, value_heads, preferred_element_type=jnp.float32
    )
    context = context.reshape(local_frames, head_width).astype(jnp.bfloat16)
    residual = (
        input_rows.astype(jnp.float32)
        + jnp.dot(context, full_weight, preferred_element_type=jnp.float32)
    ).astype(jnp.bfloat16)
    stacked_rims = with_halo(jnp.stack([residual, cotangent_rows]), (("tm", 1),), conv_reach)
    residual_ext = stacked_rims[0]
    cotangent_ext = stacked_rims[1][conv_lead : conv_lead + conv_span]
    residual_positions = (
        first_frame - conv_reach + jnp.arange(local_frames + 2 * conv_reach, dtype=jnp.int32)
    )
    residual_seg = segment_ids(starts_row, residual_positions)
    conv_seg = residual_seg[conv_lead : conv_lead + conv_span]
    own_seg = residual_seg[conv_reach : conv_reach + local_frames]
    kernel_float = full_kernel.astype(jnp.float32)
    conv_out = jnp.zeros((conv_span, residual.shape[1]), jnp.float32)
    for offset in range(KW):
        same_utt = (conv_seg == residual_seg[offset : offset + conv_span])[:, None]
        conv_out = conv_out + jnp.where(
            same_utt,
            kernel_float[offset] * residual_ext[offset : offset + conv_span].astype(jnp.float32),
            0.0,
        )
    gate_sig = jax.nn.sigmoid(conv_out)
    gated_grad = cotangent_ext.astype(jnp.float32) * gate_sig * (1.0 + conv_out * (1.0 - gate_sig))
    back_sum = cotangent_rows.astype(jnp.float32)
    own_lower = conv_lead - 1
    own_grad = gated_grad[own_lower : own_lower + local_frames]
    own_conv_seg = conv_seg[own_lower : own_lower + local_frames]
    for offset in range(KW):
        lower = KW - 1 - offset
        same_back = (conv_seg[lower : lower + local_frames] == own_seg)[:, None]
        back_sum = back_sum + jnp.where(
            same_back, kernel_float[offset] * gated_grad[lower : lower + local_frames], 0.0
        )
    products = jnp.stack(
        [
            jnp.where(
                (
                    own_conv_seg
                    == residual_seg[own_lower + offset : own_lower + offset + local_frames]
                )[:, None],
                own_grad
                * residual_ext[own_lower + offset : own_lower + offset + local_frames].astype(
                    jnp.float32
                ),
                0.0,
            )
            for offset in range(KW)
        ]
    )
    kernel_part = jnp.sum(products, axis=1)
    residual_grad = back_sum.astype(jnp.bfloat16)
    context_grad = lax.dot_general(
        residual_grad, full_weight, (((1,), (1,)), ((), ())), preferred_element_type=jnp.float32
    ).astype(jnp.bfloat16)
    grad_scale = 1.0 / math.sqrt(lax.axis_size("fsdp") * queries.shape[0] * frames_total)
    weight_part = (
        lax.dot_general(
            context, residual_grad, (((0,), (0,)), ((), ())), preferred_element_type=jnp.float32
        )
        * grad_scale
    )
    weight_share, kernel_share = (
        lax.psum_scatter(
            weight_part.astype(jnp.bfloat16), "fsdp", scatter_dimension=0, tiled=True
        ).astype(jnp.float32),
        lax.psum_scatter(
            (kernel_part * grad_scale).astype(jnp.bfloat16), "fsdp", scatter_dimension=1, tiled=True
        ).astype(jnp.float32),
    )
    weight_grad, kernel_grad = lax.psum((weight_share, kernel_share), "tm")
    return (context_grad[None], weight_grad, kernel_grad)


def solution(mesh):
    return jax.shard_map(
        shards,
        mesh=mesh,
        in_specs=(
            P("fsdp", "tm", None),
            P("fsdp", "tm", None),
            P("fsdp", "tm", None),
            P("fsdp", "tm", None),
            P("fsdp", None),
            P(None, "fsdp"),
            P("fsdp", None),
        ),
        out_specs=(P("fsdp", "tm", None), P("fsdp", None), P(None, "fsdp")),
        check_vma=False,
    )
```

profile of v0, /device:TPU:1, one launch (start us, length us, event | category | flops | bytes accessed | tf_op | source)
XLA Modules:
  0.0 252.0 jit_solution(12876443057223996696)
XLA Ops:
  8.3 2.0 collective-permute-start.1
  10.2 4.5 %collective-permute-start = (bf16[64,1536]{1,0:T(8,128)(2,1)S(1)}, bf16[64,1536]{1,0:T(8,128)(2,1)S(1)}, u32[]{:S(2)}, u32[]{:S(2)}) collective-permute-start(bf16[64,1536]{1,0:T(8,128)(2,1)S(1)} %get-tuple-element.43), channel_id=1, source_target_pairs={{0,4},{4,8},{8,12},{12,16},{16,20},{20,24},{24,28},{1,5},{5,9},{9,... | collective-permute-start | bytes 589832 | tf_op jit(solution)/shard_map/ppermute | solution.py:23
  17.5 7.2 %all_gather.6 = bf16[32,1536]{1,0:T(8,128)(2,1)S(1)} all-gather(bf16[32,384]{1,0:T(8,128)(2,1)} %param.12), channel_id=1, replica_groups=mesh['tm'=8,'fsdp'=4] {'fsdp'}, dimensions={1}, use_global_device_ids=true | all-gather | bytes 122880 | tf_op jit(solution)/shard_map/all_gather | solution.py:50
  32.5 19.9 %all-gather.2.cloned.1.call-done = bf16[768,1536]{1,0:T(8,128)(2,1)} async-done(((bf16[192,1536]{1,0:T(8,128)(2,1)}), bf16[768,1536]{1,0:T(8,128)(2,1)}) %all-gather.2.cloned.1.call-update) | async-done | bytes 2359312 | tf_op jit(solution)/shard_map/all_gather | solution.py:49
  52.4 2.2 fusion.1
  55.6 3.7 %collective-permute-start.2 = (bf16[2,31,1536]{2,1,0:T(8,128)(2,1)S(1)}, bf16[2,31,1536]{2,1,0:T(8,128)(2,1)S(1)}, u32[]{:S(2)}, u32[]{:S(2)}) collective-permute-start(bf16[2,31,1536]{2,1,0:T(8,128)(2,1)S(1)} %get-tuple-element.39), channel_id=1, source_target_pairs={{0,4},{4,8},{8,12},{12,16},{16,20},{20,24},{24,28},{1,5},{5,9},{9,... | collective-permute-start | bytes 571400 | tf_op jit(solution)/shard_map/ppermute | solution.py:23
  59.2 1.9 collective-permute-start.3
  61.8 4.4 %collective-permute-done.3 = bf16[2,31,1536]{2,1,0:T(8,128)(2,1)S(1)} collective-permute-done((bf16[2,31,1536]{2,1,0:T(8,128)(2,1)S(1)}, bf16[2,31,1536]{2,1,0:T(8,128)(2,1)S(1)}, u32[]{:S(2)}, u32[]{:S(2)}) %collective-permute-start.3) | collective-permute-done | bytes 190496 | tf_op jit(solution)/shard_map/ppermute | solution.py:24
  66.2 1.4 maximum_maximum_fusion
  67.6 1.3 pad_maximum_fusion
  68.9 6.9 %fusion.69 = f32[159,1536]{1,0:T(8,128)S(1)} fusion(bf16[2,159,1536]{2,1,0:T(8,128)(2,1)S(1)} %get-tuple-element.38, bf16[2,190,1536]{2,1,0:T(8,128)(2,1)S(1)} %pad_maximum_fusion, bf16[2,159,1536]{2,1,0:T(8,128)(2,1)S(1)} %get-tuple-element.37, f32[1536]{0:T(1024)S(1)} %get-tuple-element.4, f32[1536]{0:T(1024)S(1)} %get-tuple-element.5, ...), kind=kLoop, calls=%fused_computation.111 | loop fusion | flops 32970240 | bytes 17297216 | tf_op jit(solution)/shard_map/mul | solution.py:103
  83.9 1.2 fusion.205
  87.2 1.2 fusion.196
  88.4 1.2 fusion.193
  90.7 1.2 fusion.187
  102.0 1.2 fusion.160
  112.1 9.9 %reduce_sum.49 = f32[32,1536]{1,0:T(8,128)S(1)} reduce(f32[32,128,1536]{2,1,0:T(8,128)} %fusion.136, f32[]{:T(128)} %constant.41.clone.1), dimensions={1}, to_apply=%region_7.8 | reduce | flops 6242304 | bytes 25362436 | tf_op jit(solution)/shard_map/reduce_sum | solution.py:130
  122.7 1.9 copy.27
  124.6 6.2 %fusion.72 = bf16[128,1536]{1,0:T(8,128)(2,1)S(1)} fusion(f32[159,1536]{1,0:T(8,128)S(1)} %fusion.69, bf16[1,128,1536]{2,1,0:T(8,128)(2,1)} %param.10, f32[1536]{0:T(1024)S(1)} %get-tuple-element.4, f32[1536]{0:T(1024)} %copy-done.4, f32[1536]{0:T(1024)} %copy-done.5, f32[1536]{0:T(1024)} %copy-done.6, f32[1536]{0:T(1024)} %copy-done.7, f32[1536]{0:T(1024)} %copy-done.8, ...), kind=kLoop, calls=%fused_computation.115 | loop fusion | flops 19070976 | bytes 26152832 | tf_op jit(solution)/shard_map/convert_element_type | solution.py:131
  131.6 2.2 multiply_convert_fusion
  133.8 2.6 %fusion.6 = bf16[1,128,768]{2,1,0:T(8,128)(2,1)} fusion(bf16[128,1536]{1,0:T(8,128)(2,1)} %copy-done.1, bf16[768,1536]{1,0:T(8,128)(2,1)S(1)} %copy-done), kind=kOutput, calls=%fused_computation.12 | convolution fusion | flops 302088192 | bytes 2949120 | tf_op jit(solution)/shard_map/dot_general | solution.py:132
  136.4 11.0 %reduce-scatter.7.cloned.1.call-done = bf16[384,32]{1,0:T(8,128)(2,1)} async-done(((bf16[1536,32]{1,0:T(8,128)(2,1)}), bf16[384,32]{1,0:T(8,128)(2,1)}) %reduce-scatter.7.cloned.1.call-update) | async-done | bytes 24592
  148.4 39.8 %reduce-scatter.5.cloned.1.call-done = bf16[192,1536]{1,0:T(8,128)(2,1)} async-done(((bf16[768,1536]{1,0:T(8,128)(2,1)}), bf16[192,1536]{1,0:T(8,128)(2,1)}) %reduce-scatter.5.cloned.1.call-update) | async-done | bytes 589840 | tf_op jit(solution)/shard_map/reduce_scatter | solution.py:143
  188.2 57.2 %all-reduce.2 = (f32[192,1536]{1,0:T(8,128)}, f32[32,384]{1,0:T(8,128)}) all-reduce(bf16[192,1536]{1,0:T(8,128)(2,1)} %reduce-scatter.5.cloned.1.call-done, bf16[32,384]{1,0:T(8,128)(2,1)S(1)} %copy.28), channel_id=1, replica_groups=mesh['tm'=8,'fsdp'=4] {'tm'}, use_global_device_ids=true, to_apply=%region_6.7 | all-reduce | flops 307200 | bytes 1843200 | tf_op jit(solution)/shard_map/psum | solution.py:150
  (140 shorter events, 45.5 us)
Async XLA Ops:
  7.2 45.2 %all-gather.2.cloned.1.call-start = ((), (), s32[]{:S(2)}) async-start(), calls=%async_computation.2 | async-start | bytes 2949120 | tf_op jit(solution)/shard_map/all_gather | solution.py:49
  8.3 21.4 %collective-permute-start.1 = (bf16[64,1536]{1,0:T(8,128)(2,1)S(1)}, bf16[64,1536]{1,0:T(8,128)(2,1)S(1)}, u32[]{:S(2)}, u32[]{:S(2)}) collective-permute-start(bf16[64,1536]{1,0:T(8,128)(2,1)S(1)} %get-tuple-element.44), channel_id=1, source_target_pairs={{4,0},{8,4},{12,8},{16,12},{20,16},{24,20},{28,24},{5,1},{9,5},{13... | collective-permute-start | bytes 589832 | tf_op jit(solution)/shard_map/ppermute | solution.py:24
  10.2 19.4 %collective-permute-start = (bf16[64,1536]{1,0:T(8,128)(2,1)S(1)}, bf16[64,1536]{1,0:T(8,128)(2,1)S(1)}, u32[]{:S(2)}, u32[]{:S(2)}) collective-permute-start(bf16[64,1536]{1,0:T(8,128)(2,1)S(1)} %get-tuple-element.43), channel_id=1, source_target_pairs={{0,4},{4,8},{8,12},{12,16},{16,20},{20,24},{24,28},{1,5},{5,9},{9,... | collective-permute-start | bytes 589832 | tf_op jit(solution)/shard_map/ppermute | solution.py:23
  14.8 132.6 %reduce-scatter.7.cloned.1.call-start = ((), (), s32[]{:S(2)}) async-start(), calls=%async_computation.4 | async-start | bytes 491520
  25.0 56.3 %copy-start.4 = (f32[1536]{0:T(1024)}, f32[1536]{0:T(1024)S(1)}, u32[]{:S(2)}) copy-start(f32[1536]{0:T(1024)S(1)} %get-tuple-element.5) | copy-start | bytes 18436
  25.0 56.3 %copy-start.5 = (f32[1536]{0:T(1024)}, f32[1536]{0:T(1024)S(1)}, u32[]{:S(2)}) copy-start(f32[1536]{0:T(1024)S(1)} %get-tuple-element.6) | copy-start | bytes 18436
  25.0 56.3 %copy-start.6 = (f32[1536]{0:T(1024)}, f32[1536]{0:T(1024)S(1)}, u32[]{:S(2)}) copy-start(f32[1536]{0:T(1024)S(1)} %get-tuple-element.7) | copy-start | bytes 18436
  25.1 56.3 %copy-start.7 = (f32[1536]{0:T(1024)}, f32[1536]{0:T(1024)S(1)}, u32[]{:S(2)}) copy-start(f32[1536]{0:T(1024)S(1)} %get-tuple-element.8) | copy-start | bytes 18436
  25.1 56.3 %copy-start.8 = (f32[1536]{0:T(1024)}, f32[1536]{0:T(1024)S(1)}, u32[]{:S(2)}) copy-start(f32[1536]{0:T(1024)S(1)} %get-tuple-element.9) | copy-start | bytes 18436
  25.1 56.3 %copy-start.9 = (f32[1536]{0:T(1024)}, f32[1536]{0:T(1024)S(1)}, u32[]{:S(2)}) copy-start(f32[1536]{0:T(1024)S(1)} %get-tuple-element.10) | copy-start | bytes 18436
  25.1 56.3 %copy-start.10 = (f32[1536]{0:T(1024)}, f32[1536]{0:T(1024)S(1)}, u32[]{:S(2)}) copy-start(f32[1536]{0:T(1024)S(1)} %get-tuple-element.11) | copy-start | bytes 18436
  25.1 56.3 %copy-start.11 = (f32[1536]{0:T(1024)}, f32[1536]{0:T(1024)S(1)}, u32[]{:S(2)}) copy-start(f32[1536]{0:T(1024)S(1)} %get-tuple-element.12) | copy-start | bytes 18436
  25.1 56.3 %copy-start.12 = (f32[1536]{0:T(1024)}, f32[1536]{0:T(1024)S(1)}, u32[]{:S(2)}) copy-start(f32[1536]{0:T(1024)S(1)} %get-tuple-element.13) | copy-start | bytes 18436
  25.1 56.3 %copy-start.13 = (f32[1536]{0:T(1024)}, f32[1536]{0:T(1024)S(1)}, u32[]{:S(2)}) copy-start(f32[1536]{0:T(1024)S(1)} %get-tuple-element.14) | copy-start | bytes 18436
  25.1 56.3 %copy-start.14 = (f32[1536]{0:T(1024)}, f32[1536]{0:T(1024)S(1)}, u32[]{:S(2)}) copy-start(f32[1536]{0:T(1024)S(1)} %get-tuple-element.15) | copy-start | bytes 18436
  25.1 56.3 %copy-start.15 = (f32[1536]{0:T(1024)}, f32[1536]{0:T(1024)S(1)}, u32[]{:S(2)}) copy-start(f32[1536]{0:T(1024)S(1)} %get-tuple-element.16) | copy-start | bytes 18436
  25.1 56.3 %copy-start.16 = (f32[1536]{0:T(1024)}, f32[1536]{0:T(1024)S(1)}, u32[]{:S(2)}) copy-start(f32[1536]{0:T(1024)S(1)} %get-tuple-element.17) | copy-start | bytes 18436
  25.2 56.3 %copy-start.17 = (f32[1536]{0:T(1024)}, f32[1536]{0:T(1024)S(1)}, u32[]{:S(2)}) copy-start(f32[1536]{0:T(1024)S(1)} %get-tuple-element.18) | copy-start | bytes 18436
  25.2 56.3 %copy-start.18 = (f32[1536]{0:T(1024)}, f32[1536]{0:T(1024)S(1)}, u32[]{:S(2)}) copy-start(f32[1536]{0:T(1024)S(1)} %get-tuple-element.19) | copy-start | bytes 18436
  25.2 56.3 %copy-start.19 = (f32[1536]{0:T(1024)}, f32[1536]{0:T(1024)S(1)}, u32[]{:S(2)}) copy-start(f32[1536]{0:T(1024)S(1)} %get-tuple-element.20) | copy-start | bytes 18436
  25.2 56.3 %copy-start.20 = (f32[1536]{0:T(1024)}, f32[1536]{0:T(1024)S(1)}, u32[]{:S(2)}) copy-start(f32[1536]{0:T(1024)S(1)} %get-tuple-element.21) | copy-start | bytes 18436
  55.6 6.3 %collective-permute-start.2 = (bf16[2,31,1536]{2,1,0:T(8,128)(2,1)S(1)}, bf16[2,31,1536]{2,1,0:T(8,128)(2,1)S(1)}, u32[]{:S(2)}, u32[]{:S(2)}) collective-permute-start(bf16[2,31,1536]{2,1,0:T(8,128)(2,1)S(1)} %get-tuple-element.39), channel_id=1, source_target_pairs={{0,4},{4,8},{8,12},{12,16},{16,20},{20,24},{24,28},{1,5},{5,9},{9,... | collective-permute-start | bytes 571400 | tf_op jit(solution)/shard_map/ppermute | solution.py:23
  59.2 7.0 %collective-permute-start.3 = (bf16[2,31,1536]{2,1,0:T(8,128)(2,1)S(1)}, bf16[2,31,1536]{2,1,0:T(8,128)(2,1)S(1)}, u32[]{:S(2)}, u32[]{:S(2)}) collective-permute-start(bf16[2,31,1536]{2,1,0:T(8,128)(2,1)S(1)} %get-tuple-element.40), channel_id=1, source_target_pairs={{4,0},{8,4},{12,8},{16,12},{20,16},{24,20},{28,24},{5,1},{9,5},{13... | collective-permute-start | bytes 571400 | tf_op jit(solution)/shard_map/ppermute | solution.py:24
  124.6 63.6 %reduce-scatter.5.cloned.1.call-start = ((), (), s32[]{:S(2)}) async-start(), calls=%async_computation.3 | async-start | bytes 2949120 | tf_op jit(solution)/shard_map/reduce_scatter | solution.py:143
  (17 other events, 785.8 us)
Sparse Core Ops, SparseCore 0:
  14.9 37.3 all-gather.1
  124.7 22.6 reduce-scatter.6
  150.4 37.6 reduce-scatter.4
where the time goes:
time: 256 us; the launch traced here: 252 us
  waiting for transfers between devices  75.8 us (30%)
  other arithmetic  70.1 us (27%)
  blocking collectives  64.4 us (25%)
  between operations  14.5 us (6%)
  starting transfers between devices  12.2 us (5%)
  matrix products  8.24 us (3%)
  local copies, waits for them, and re-layouts  6.79 us (3%)
    psum x1, blocking collectives, shards(): weight_grad, kernel_grad = lax.psum((weight_share, kernel_share), 'tm')  57.2 us
    reduce_scatter x1, waiting for transfers between devices, shards(): lax.psum_scatter(weight_part.astype(jnp.bfloat16), 'fsdp', scatter_dimens...  39.8 us
    unnamed x31, other arithmetic  34.9 us
    all_gather x1, waiting for transfers between devices, shards(): lax.all_gather(out_weight, 'fsdp', axis=0, tiled=True)  19.9 us
    unnamed x4, waiting for transfers between devices  11.1 us
    reduce_sum x1, other arithmetic, shards(): kernel_part = jnp.sum(products, axis=1)  9.91 us
    ppermute x2, starting transfers between devices, with_halo(): before = lax.ppermute(last, axis, up)  8.22 us
    all_gather x1, blocking collectives, shards(): lax.all_gather(conv_kernel, 'fsdp', axis=1, tiled=True)  7.2 us
  transfers between devices with their start and end apart: 7, of which 5 were waited for; matrix products, arithmetic and copies ran while one was open for 9% of the time, Pallas kernels for 0%

commit v1 on v0

--- a/solution.py
+++ b/solution.py
@@ -1,8 +1,11 @@
+import functools
 import math
 
 import jax
 import jax.numpy as jnp
 from jax import lax
+from jax.experimental import pallas as pl
+from jax.experimental.pallas import tpu as pltpu
 from jax.sharding import PartitionSpec as P
 
 HEADS_W = 8
@@ -151,9 +154,538 @@
     return (context_grad[None], weight_grad, kernel_grad)
 
 
+MESH = pl.DeviceIdType.MESH
+KEY_PAD = 96
+ROW_PAD = 32
+COT_PAD = 16
+BLOCK = 64
+LANES = 128
+
+
+def dot(a, b):
+    return jnp.dot(a, b, preferred_element_type=jnp.float32)
+
+
+def dot_t(a, b):
+    return lax.dot_general(a, b, (((1,), (1,)), ((), ())), preferred_element_type=jnp.float32)
+
+
+def block_kernel(
+    nt, nf,
+    starts_ref, q_ref, kv_ref, in_ref, cot_ref, w_ref, ck_ref,
+    cg_ref, wg_ref, kg_ref,
+    kvx, qx, inx, cotx, wfull, kall, kf, seg, m1, ctx, ctx_t, res, gs, rg, kgs,
+    part, own, asrc, abuf, bsrc, bbuf, fsum, csrc, cbuf, gbuf,
+    kgsrc, kgb, kgcs, kgc, kgds, kgd,
+    hs, hr, ws, wr, fs, fr, ks, kr, as_, ar, bs, br, cs, cr, gsn, grc, ds_, dr,
+    kbs, kbr, kcs, kcr, kds, kdr,
+):
+    nz = nt // 2
+    t = lax.axis_index("tm")
+    f = lax.axis_index("fsdp")
+    z = lax.div(t, 2)
+    c = lax.rem(t, 2)
+    sib = t + 1 - 2 * c
+    rows = q_ref.shape[0]
+    shard = w_ref.shape[0]
+    half = shard // 2
+    width = in_ref.shape[1]
+    head_width = q_ref.shape[1]
+    head_size = head_width // HEADS_W
+    chunks = width // LANES
+    per_shard = chunks // nf
+    chunk_w = width // nz
+    per_piece = chunks // nz
+    ext = rows + 2 * ROW_PAD
+    span = rows + 2 * COT_PAD
+    first = t * rows
+    total = nt * rows
+
+    def other_f(i):
+        return lax.rem(f + i, nf)
+
+    def from_f(i):
+        return lax.rem(f + nf - i, nf)
+
+    def other_z(i):
+        return lax.rem(z + i, nz)
+
+    def copy(src, dst, send, recv, tm, fsdp):
+        return pltpu.make_async_remote_copy(
+            src_ref=src, dst_ref=dst, send_sem=send, recv_sem=recv,
+            device_id={"tm": tm, "fsdp": fsdp}, device_id_type=MESH,
+        )
+
+    barrier = pltpu.get_barrier_semaphore()
+
+    def greet(tm, fsdp):
+        pl.semaphore_signal(
+            barrier, inc=1, device_id={"tm": tm, "fsdp": fsdp}, device_id_type=MESH
+        )
+
+    for i in range(1, nf):
+        greet(t, other_f(i))
+    for i in range(1, nz):
+        greet(2 * other_z(i) + c, f)
+
+    @pl.when(t > 0)
+    def _():
+        greet(t - 1, f)
+
+    @pl.when(t < nt - 1)
+    def _():
+        greet(t + 1, f)
+
+    near = jnp.minimum(t, 1) + jnp.minimum(nt - 1 - t, 1)
+    pl.semaphore_wait(barrier, nf - 1 + nz - 1 + near)
+
+    halo = ((kv_ref, kvx, KEY_PAD), (q_ref, qx, ROW_PAD), (in_ref, inx, ROW_PAD), (cot_ref, cotx, COT_PAD))
+
+    def up_copy(n):
+        src, dst, pad = halo[n]
+        return copy(
+            src.at[pl.ds(rows - pad, pad)], dst.at[pl.ds(0, pad)], hs.at[0, n], hr.at[0, n], t + 1, f
+        )
+
+    def down_copy(n):
+        src, dst, pad = halo[n]
+        return copy(
+            src.at[pl.ds(0, pad)], dst.at[pl.ds(pad + rows, pad)], hs.at[1, n], hr.at[1, n], t - 1, f
+        )
+
+    @pl.when(t < nt - 1)
+    def _():
+        for n in range(4):
+            up_copy(n).start()
+
+    @pl.when(t > 0)
+    def _():
+        for n in range(4):
+            down_copy(n).start()
+
+    def rows_of(owner, core):
+        return pl.ds(pl.multiple_of(owner * shard + core * half, 16), half)
+
+    w_copies = [
+        copy(
+            w_ref.at[pl.ds(pl.multiple_of(c * half, 16), half)], wfull.at[rows_of(f, c)],
+            ws.at[i], wr.at[i], t, other_f(i),
+        )
+        for i in range(1, nf)
+    ]
+    k_copies = [
+        copy(ck_ref, kall.at[f], ks.at[i], kr.at[i], t, other_f(i)) for i in range(1, nf)
+    ]
+    for w_copy in w_copies:
+        w_copy.start()
+    for k_copy in k_copies:
+        k_copy.start()
+
+    @pl.when(t == 0)
+    def _():
+        for src, dst, pad in halo:
+            dst[0:pad] = jnp.zeros((pad, dst.shape[1]), dst.dtype)
+
+    @pl.when(t == nt - 1)
+    def _():
+        for src, dst, pad in halo:
+            dst[pad + rows : 2 * pad + rows] = jnp.zeros((pad, dst.shape[1]), dst.dtype)
+
+    for src, dst, pad in halo:
+        dst[pad : pad + rows] = src[...]
+    wfull[pl.ds(pl.multiple_of(f * shard, 16), shard)] = w_ref[...]
+    kall[f] = ck_ref[...]
+
+    utts = starts_ref.shape[1]
+
+    def segments(positions):
+        found = jnp.full(positions.shape, -1.0, jnp.float32)
+        for u in range(utts):
+            found = found + jnp.where(starts_ref[0, u] <= positions, 1.0, 0.0)
+        return jnp.where(positions < total, found, -1.0)
+
+    seg[...] = segments(lax.broadcasted_iota(jnp.int32, (ext, LANES), 0) + (first - ROW_PAD))
+
+    for k in range(KW + 1):
+        m1[k] = jnp.where(seg[k : k + span] == seg[COT_PAD : COT_PAD + span], 1.0, 0.0)
+
+    @pl.when(t > 0)
+    def _():
+        for n in range(4):
+            up_copy(n).wait_recv()
+
+    @pl.when(t < nt - 1)
+    def _():
+        for n in range(4):
+            down_copy(n).wait_recv()
+
+    keys = 2 * LANES
+    key_rows = rows + 2 * KEY_PAD
+    scale = 1.0 / math.sqrt(head_size)
+    lane = lax.broadcasted_iota(jnp.int32, (1, keys), 1)
+    for b in range(ext // BLOCK):
+        start = min(BLOCK * b, key_rows - keys)
+        key_seg = segments(lane + (first - KEY_PAD + start))
+        query_seg = seg[BLOCK * b : BLOCK * (b + 1)]
+        query_seg = jnp.concatenate([query_seg, query_seg], axis=1)
+        gap = (
+            lax.broadcasted_iota(jnp.int32, (BLOCK, keys), 1)
+            - lax.broadcasted_iota(jnp.int32, (BLOCK, keys), 0)
+            + (start - KEY_PAD - BLOCK * b + ROW_PAD)
+        )
+        allowed = (gap >= -(WIN // 2)) & (gap <= WIN // 2) & (query_seg == key_seg)
+        bias = jnp.where(allowed, 0.0, masked_score)
+        bias = jnp.concatenate([bias, bias], axis=0)
+        for g in range(HEADS_W // 4):
+            pairs = []
+            for p in range(2):
+                base = 4 * head_size * g + LANES * p
+                lower = (2 * head_size - LANES) * p
+                middle, upper = lower + head_size, lower + 2 * head_size
+                in_a = jnp.where((lane >= lower) & (lane < middle), 1.0, 0.0)
+                in_b = jnp.where((lane >= middle) & (lane < upper), 1.0, 0.0)
+                query = qx[BLOCK * b : BLOCK * (b + 1), base : base + keys]
+                query = jnp.concatenate(
+                    [query * in_a.astype(jnp.bfloat16), query * in_b.astype(jnp.bfloat16)], axis=0
+                )
+                scores = dot_t(query, kvx[start : start + keys, base : base + keys]) * scale + bias
+                weights = jnp.exp(scores - jnp.max(scores, axis=1, keepdims=True))
+                probs = (weights / jnp.sum(weights, axis=1, keepdims=True)).astype(jnp.bfloat16)
+                value = dot(
+                    probs,
+                    kvx[start : start + keys, head_width + base : head_width + base + keys],
+                )
+                pairs.append(value[:BLOCK] * in_a + value[BLOCK:] * in_b)
+            joined = jnp.concatenate(
+                [
+                    pairs[0][:, :LANES],
+                    pairs[0][:, LANES:] + pairs[1][:, :LANES],
+                    pairs[1][:, LANES:],
+                ],
+                axis=1,
+            )
+            ctx[BLOCK * b : BLOCK * (b + 1), 4 * head_size * g : 4 * head_size * (g + 1)] = (
+                joined.astype(jnp.bfloat16)
+            )
+    ctx_t[...] = ctx[ROW_PAD : ROW_PAD + rows].astype(jnp.float32).T.astype(jnp.bfloat16)
+
+    def forward(i):
+        piece = wfull.at[rows_of(from_f(i), c)]
+        return copy(piece, piece, fs.at[i], fr.at[i], sib, f)
+
+    for i in range(1, nf):
+        w_copies[i - 1].wait_recv()
+        forward(i).start()
+    for i in range(1, nf):
+        k_copies[i - 1].wait_recv()
+    for s in range(nf):
+        for i in range(per_shard):
+            kf[s * per_shard + i] = kall[s, :, LANES * i : LANES * (i + 1)].astype(jnp.float32)
+    for i in range(1, nf):
+        forward(i).wait_recv()
+
+    for j in range(nz):
+        columns = slice(chunk_w * j, chunk_w * (j + 1))
+        out = inx[:, columns].astype(jnp.float32) + dot(ctx[...], wfull[:, columns])
+        out = out.astype(jnp.bfloat16).astype(jnp.float32)
+        for i in range(per_piece):
+            res[per_piece * j + i] = out[:, LANES * i : LANES * (i + 1)]
+
+    def conv_chunk(n, carry):
+        columns = pl.ds(pl.multiple_of(n * LANES, LANES), LANES)
+        conv = jnp.zeros((span, LANES), jnp.float32)
+        for b in range(8):
+            shifted = res[n, pl.ds(b, span + 24), :]
+            for a in range(KW // 8):
+                k = 8 * a + b
+                conv = conv + m1[k] * (kf[n, k : k + 1, :] * shifted[8 * a : 8 * a + span])
+        sig = jax.nn.sigmoid(conv)
+        cot = cotx[:, columns].astype(jnp.float32)
+        gs[...] = cot * sig * (1.0 + conv * (1.0 - sig))
+        back = cot_ref[:, columns].astype(jnp.float32)
+        mid = slice(COT_PAD, COT_PAD + rows)
+        for b in range(8):
+            low = 8 if b == 0 else 0
+            shifted = gs[b + low : b + low + rows + 24]
+            for a in range(KW // 8):
+                o = 8 * a + b + low
+                k = KW - o
+                back = back + m1[o, mid] * (kf[n, k : k + 1, :] * shifted[8 * a : 8 * a + rows])
+        rg[:, columns] = back.astype(jnp.bfloat16)
+        grad = gs[mid]
+        for b in range(8):
+            shifted = res[n, pl.ds(COT_PAD + b, rows + 24), :]
+            for a in range(KW // 8):
+                k = 8 * a + b
+                prod = m1[k, mid] * grad * shifted[8 * a : 8 * a + rows]
+                prod = jnp.sum(prod.reshape(rows // 8, 8, LANES), axis=0)
+                kgs[n, k : k + 1, :] = jnp.sum(prod, axis=0, keepdims=True)
+        return carry
+
+    def a_copy(j):
+        return copy(asrc.at[j], abuf.at[j], as_.at[j], ar.at[j], sib, f)
+
+    def b_copy(j, i):
+        return copy(
+            bsrc.at[j, other_f(i)], bbuf.at[j, i], bs.at[j, i], br.at[j, i], t, other_f(i)
+        )
+
+    def c_copy(j):
+        return copy(csrc.at[j], cbuf.at[z], cs.at[j], cr.at[z], 2 * j + c, f)
+
+    def finish_a(j):
+        a_copy(j).wait_recv()
+        for s in range(nf):
+            bsrc[j, s] = (own[j, s] + abuf[j, s].astype(jnp.float32)).astype(jnp.bfloat16)
+        for i in range(1, nf):
+            b_copy(j, i).start()
+
+    def finish_b(j):
+        acc = own[j, f] + abuf[j, f].astype(jnp.float32)
+        for i in range(1, nf):
+            b_copy(j, i).wait_recv()
+            acc = acc + bbuf[j, i].astype(jnp.float32)
+
+        @pl.when(z == j)
+        def _():
+            fsum[...] = acc
+
+        @pl.when(z != j)
+        def _():
+            csrc[j] = acc.astype(jnp.bfloat16)
+            c_copy(j).start()
+
+    for j in range(nz):
+        lax.fori_loop(per_piece * j, per_piece * (j + 1), conv_chunk, 0)
+        part[...] = dot(ctx_t[...], rg[:, chunk_w * j : chunk_w * (j + 1)])
+        for s in range(nf):
+            own[j, s] = part[rows_of(s, c)]
+            asrc[j, s] = part[rows_of(s, 1 - c)].astype(jnp.bfloat16)
+        a_copy(j).start()
+        if j >= 1:
+            finish_a(j - 1)
+        if j >= 2:
+            finish_b(j - 2)
+
+    def kb_copy(i):
+        return copy(kgsrc.at[other_f(i)], kgb.at[i], kbs.at[i], kbr.at[i], t, other_f(i))
+
+    for s in range(nf):
+        for i in range(per_shard):
+            kgsrc[s, i] = kgs[s * per_shard + i].astype(jnp.bfloat16)
+    for i in range(1, nf):
+        kb_copy(i).start()
+    finish_a(nz - 1)
+    if nz >= 2:
+        finish_b(nz - 2)
+    cg_ref[...] = dot_t(rg[...], wfull[...]).astype(jnp.bfloat16)
+
+    kg_sum = kgs[pl.ds(f * per_shard, per_shard)]
+    for i in range(1, nf):
+        kb_copy(i).wait_recv()
+        kg_sum = kg_sum + kgb[i].astype(jnp.float32)
+    kgcs[...] = kg_sum.astype(jnp.bfloat16)
+
+    def kc_copy(i):
+        return copy(kgcs, kgc.at[z], kcs.at[i], kcr.at[z], 2 * other_z(i) + c, f)
+
+    def kc_from(i):
+        s = other_z(i)
+        return copy(kgcs, kgc.at[s], kcs.at[i], kcr.at[s], 2 * s + c, f)
+
+    for i in range(1, nz):
+        kc_copy(i).start()
+    kgc[z] = kgcs[...]
+    finish_b(nz - 1)
+
+    def c_from(i):
+        s = other_z(i)
+        return copy(csrc.at[0], cbuf.at[s], cs.at[0], cr.at[s], 2 * s + c, f)
+
+    final = fsum[...]
+    for i in range(1, nz):
+        c_from(i).wait_recv()
+        final = final + cbuf[other_z(i)].astype(jnp.float32)
+    gbuf[c, z] = final.astype(jnp.bfloat16)
+
+    def g_copy(i):
+        piece = gbuf.at[c, z]
+        return copy(piece, piece, gsn.at[i], grc.at[z], 2 * other_z(i) + c, f)
+
+    def g_from(i):
+        s = other_z(i)
+        piece = gbuf.at[c, s]
+        return copy(piece, piece, gsn.at[i], grc.at[s], 2 * s + c, f)
+
+    def d_copy(s):
+        piece = gbuf.at[c, s]
+        return copy(piece, piece, ds_.at[s], dr.at[s], sib, f)
+
+    def d_from(s):
+        piece = gbuf.at[1 - c, s]
+        return copy(piece, piece, ds_.at[s], dr.at[s], sib, f)
+
+    for i in range(1, nz):
+        g_copy(i).start()
+    d_copy(z).start()
+
+    for i in range(1, nz):
+        kc_from(i).wait_recv()
+    kg_z = kgc[0].astype(jnp.float32)
+    for s in range(1, nz):
+        kg_z = kg_z + kgc[s].astype(jnp.float32)
+    kgds[...] = kg_z.astype(jnp.bfloat16)
+    kd_copy = copy(kgds, kgd, kds, kdr, sib, f)
+    kd_copy.start()
+
+    for i in range(1, nz):
+        g_from(i).wait_recv()
+        d_copy(other_z(i)).start()
+    kd_copy.wait_recv()
+    kg_all = kgds[...].astype(jnp.float32) + kgd[...].astype(jnp.float32)
+    for i in range(per_shard):
+        kg_ref[:, LANES * i : LANES * (i + 1)] = kg_all[i]
+    mine = pl.ds(pl.multiple_of(c * half, 16), half)
+    theirs = pl.ds(pl.multiple_of((1 - c) * half, 16), half)
+    for s in range(nz):
+        wg_ref[mine, chunk_w * s : chunk_w * (s + 1)] = gbuf[c, s]
+    for i in range(nz):
+        d_from(other_z(i)).wait_recv()
+    for s in range(nz):
+        wg_ref[theirs, chunk_w * s : chunk_w * (s + 1)] = gbuf[1 - c, s]
+
+    @pl.when(t < nt - 1)
+    def _():
+        for n in range(4):
+            up_copy(n).wait_send()
+
+    @pl.when(t > 0)
+    def _():
+        for n in range(4):
+            down_copy(n).wait_send()
+
+    for i in range(1, nf):
+        w_copies[i - 1].wait_send()
+        k_copies[i - 1].wait_send()
+        forward(i).wait_send()
+        kb_copy(i).wait_send()
+    for j in range(nz):
+        a_copy(j).wait_send()
+        for i in range(1, nf):
+            b_copy(j, i).wait_send()
+
+        @pl.when(z != j)
+        def _():
+            c_copy(j).wait_send()
+
+    for i in range(1, nz):
+        kc_copy(i).wait_send()
+        g_copy(i).wait_send()
+    for i in range(nz):
+        d_copy(other_z(i)).wait_send()
+    kd_copy.wait_send()
+
+
+def fused(nt, nf, queries, keys_values, inputs, cotangent, out_weight, conv_kernel, utt_starts):
+    rows, head_width = queries.shape[1:]
+    width = inputs.shape[2]
+    nz = nt // 2
+    shard = out_weight.shape[0]
+    half = shard // 2
+    chunks = width // LANES
+    per_shard = chunks // nf
+    chunk_w = width // nz
+    ext = rows + 2 * ROW_PAD
+    span = rows + 2 * COT_PAD
+    bf16, f32 = jnp.bfloat16, jnp.float32
+    dma = pltpu.SemaphoreType.DMA
+    vmem = pl.BlockSpec(memory_space=pltpu.VMEM)
+    scratch = [
+        ((rows + 2 * KEY_PAD, 2 * head_width), bf16),
+        ((ext, head_width), bf16),
+        ((ext, width), bf16),
+        ((span, width), bf16),
+        ((head_width, width), bf16),
+        ((nf, KW, width // nf), bf16),
+        ((chunks, KW, LANES), f32),
+        ((ext, LANES), f32),
+        ((KW + 1, span, LANES), f32),
+        ((ext, head_width), bf16),
+        ((head_width, rows), bf16),
+        ((chunks, ext, LANES), f32),
+        ((span, LANES), f32),
+        ((rows, width), bf16),
+        ((chunks, KW, LANES), f32),
+        ((head_width, chunk_w), f32),
+        ((nz, nf, half, chunk_w), f32),
+        ((nz, nf, half, chunk_w), bf16),
+        ((nz, nf, half, chunk_w), bf16),
+        ((nz, nf, half, chunk_w), bf16),
+        ((nz, nf, half, chunk_w), bf16),
+        ((half, chunk_w), f32),
+        ((nz, half, chunk_w), bf16),
+        ((nz, half, chunk_w), bf16),
+        ((2, nz, half, chunk_w), bf16),
+        ((nf, per_shard, KW, LANES), bf16),
+        ((nf, per_shard, KW, LANES), bf16),
+        ((per_shard, KW, LANES), bf16),
+        ((nz, per_shard, KW, LANES), bf16),
+        ((per_shard, KW, LANES), bf16),
+        ((per_shard, KW, LANES), bf16),
+    ]
+    sems = [
+        (2, 4), (2, 4), (nf,), (nf,), (nf,), (nf,), (nf,), (nf,), (nz,), (nz,), (nz, nf), (nz, nf),
+        (nz,), (nz,), (nz,), (nz,), (nz,), (nz,), (nf,), (nf,), (nz,), (nz,),
+    ]
+    context_grad, weight_grad, kernel_grad = pl.pallas_call(
+        functools.partial(block_kernel, nt, nf),
+        out_shape=(
+            jax.ShapeDtypeStruct((rows, head_width), bf16),
+            jax.ShapeDtypeStruct((shard, width), bf16),
+            jax.ShapeDtypeStruct((KW, width // nf), f32),
+        ),
+        in_specs=[pl.BlockSpec(memory_space=pltpu.SMEM)] + [vmem] * 6,
+        out_specs=(vmem, vmem, vmem),
+        scratch_shapes=[pltpu.VMEM(*s) for s in scratch]
+        + [dma(s) for s in sems]
+        + [dma, dma],
+        compiler_params=pltpu.CompilerParams(
+            collective_id=0, has_side_effects=True, vmem_limit_bytes=48 * 1024 * 1024
+        ),
+    )(utt_starts, queries[0], keys_values[0], inputs[0], cotangent[0], out_weight, conv_kernel)
+    grad_scale = 1.0 / math.sqrt(nf * queries.shape[0] * nt * rows)
+    return (
+        context_grad[None],
+        weight_grad.astype(jnp.float32) * grad_scale,
+        kernel_grad * grad_scale,
+    )
+
+
+def fits(nt, nf, queries, keys_values, inputs, cotangent, out_weight, conv_kernel, utt_starts):
+    rows, head_width = queries.shape[1:]
+    width = inputs.shape[2]
+    return (
+        queries.shape[0] == 1
+        and rows == 2 * BLOCK
+        and nt % 2 == 0
+        and nt >= 4
+        and (width // LANES) % (nt // 2) == 0
+        and (width // LANES) % nf == 0
+        and out_weight.shape[0] % 32 == 0
+        and head_width * LANES == HEADS_W * 96 * LANES
+    )
+
+
 def solution(mesh):
+    nt, nf = mesh.shape["tm"], mesh.shape["fsdp"]
+
+    def body(*arrays):
+        if fits(nt, nf, *arrays):
+            return fused(nt, nf, *arrays)
+        return shards(*arrays)
+
     return jax.shard_map(
-        shards,
+        body,
         mesh=mesh,
         in_specs=(
             P("fsdp", "tm", None),

time: 256 us -> 73.5 us (0.29); the launches traced: 252 us -> 73.1 us
  waiting for transfers between devices: 75.8 us -> 0 us
  other arithmetic: 70.1 us -> 1.77 us
  blocking collectives: 64.4 us -> 0 us
  Pallas kernels: 0 us -> 63.6 us
  between operations: 14.5 us -> 0.66 us
  starting transfers between devices: 12.2 us -> 0 us
  matrix products: 8.24 us -> 0 us
    pallas_call x0 -> x1, Pallas kernels: none -> 63.6 us  [fused(): pl.pallas_call(functools.partial(block_kernel, nt, nf), out_shape=(jax.Sh...]
    psum x1 -> x0, blocking collectives: 57.2 us -> none  [shards(): weight_grad, kernel_grad = lax.psum((weight_share, kernel_share), 'tm')]
    reduce_scatter x1 -> x0, waiting for transfers between devices: 39.8 us -> none  [shards(): lax.psum_scatter(weight_part.astype(jnp.bfloat16), 'fsdp', scatter_dimens...]
    unnamed x31 -> x0, other arithmetic: 34.9 us -> none
    all_gather x1 -> x0, waiting for transfers between devices: 19.9 us -> none  [shards(): lax.all_gather(out_weight, 'fsdp', axis=0, tiled=True)]
    reduce_sum x4 -> x0, other arithmetic: 12.1 us -> none  [the longest x1 9.91 us: shards(): kernel_part = jnp.sum(products, axis=1)]
    ppermute x4 -> x0, starting transfers between devices: 12.1 us -> none  [the longest x2 8.22 us: with_halo(): before = lax.ppermute(last, axis, up)]
    unnamed x4 -> x0, waiting for transfers between devices: 11.1 us -> none
  transfers between devices with their start and end apart: 7 -> 0, of which waited for: 5 -> 0; matrix products, arithmetic and copies ran while one was open for 9% -> 0% of each run, Pallas kernels for 0% -> 0%
where the time goes in v1:
time: 73.5 us; the launch traced here: 73.1 us
  Pallas kernels  63.6 us (87%)
  local copies, waits for them, and re-layouts  7.04 us (10%)
  other arithmetic  1.77 us (2%)
    pallas_call x1, Pallas kernels, fused(): pl.pallas_call(functools.partial(block_kernel, nt, nf), out_shape=(jax.Sh...  63.6 us
    unnamed x15, local copies, waits for them, and re-layouts  7.04 us

profile of v1, /device:TPU:1, one launch (start us, length us, event | category | flops | bytes accessed | tf_op | source)
XLA Modules:
  0.0 73.1 jit_solution(17661008689605488431)
XLA Ops:
  0.6 0.0 copy-start
  0.6 1.1 %copy-done = bf16[192,1536]{1,0:T(8,128)(2,1)S(1)} copy-done((bf16[192,1536]{1,0:T(8,128)(2,1)S(1)}, bf16[192,1536]{1,0:T(8,128)(2,1)}, u32[]{:S(2)}) %copy-start) | copy-done | bytes 589848
  1.7 0.0 copy-start.1
  1.7 1.0 %copy-done.1 = bf16[1,128,1536]{2,1,0:T(8,128)(2,1)S(1)} copy-done((bf16[1,128,1536]{2,1,0:T(8,128)(2,1)S(1)}, bf16[1,128,1536]{2,1,0:T(8,128)(2,1)}, u32[]{:S(2)}) %copy-start.1) | copy-done | bytes 393240
  2.7 0.0 copy-start.2
  2.7 1.0 %copy-done.2 = bf16[1,128,1536]{2,1,0:T(8,128)(2,1)S(1)} copy-done((bf16[1,128,1536]{2,1,0:T(8,128)(2,1)S(1)}, bf16[1,128,1536]{2,1,0:T(8,128)(2,1)}, u32[]{:S(2)}) %copy-start.2) | copy-done | bytes 393240
  3.7 0.0 copy-start.3
  3.7 1.0 %copy-done.3 = bf16[1,128,1536]{2,1,0:T(8,128)(2,1)S(1)} copy-done((bf16[1,128,1536]{2,1,0:T(8,128)(2,1)S(1)}, bf16[1,128,1536]{2,1,0:T(8,128)(2,1)}, u32[]{:S(2)}) %copy-start.3) | copy-done | bytes 393240
  4.7 0.0 copy-start.4
  4.7 0.9 %copy-done.4 = bf16[1,128,768]{2,1,0:T(8,128)(2,1)S(1)} copy-done((bf16[1,128,768]{2,1,0:T(8,128)(2,1)S(1)}, bf16[1,128,768]{2,1,0:T(8,128)(2,1)}, u32[]{:S(2)}) %copy-start.4) | copy-done | bytes 196632
  5.6 0.0 copy-start.5
  5.6 0.7 %copy-done.5 = bf16[32,384]{1,0:T(8,128)(2,1)S(1)} copy-done((bf16[32,384]{1,0:T(8,128)(2,1)S(1)}, bf16[32,384]{1,0:T(8,128)(2,1)}, u32[]{:S(2)}) %copy-start.5) | copy-done | bytes 24600
  6.4 0.0 copy-start.6
  6.4 0.7 copy-done.6
  7.0 63.6 %shard_map.94 = (bf16[128,768]{1,0:T(8,128)(2,1)S(1)}, bf16[192,1536]{1,0:T(8,128)(2,1)S(1)}, f32[32,384]{1,0:T(8,128)S(1)}) custom-call(s32[1,16]{1,0:T(1,128)S(1)} %copy-done.6, bf16[128,768]{1,0:T(8,128)(2,1)S(1)} %bitcast.8, bf16[128,1536]{1,0:T(8,128)(2,1)S(1)} %bitcast.5, bf16[128,1536]{1,0:T(8,128)(2,1)S(1)} %bitcast.6, ...), custom_call_target="tpu_custom_call" | custom-call | tf_op jit(solution)/shard_map/pallas_call | solution.py:640
  70.6 0.6 broadcast_multiply_fusion
  71.3 1.1 %convert_multiply_fusion = f32[192,1536]{1,0:T(8,128)} fusion(bf16[192,1536]{1,0:T(8,128)(2,1)S(1)} %get-tuple-element.7), kind=kLoop, calls=%fused_computation | loop fusion | flops 589824 | bytes 1769472 | tf_op jit(solution)/shard_map/mul | solution.py:659
  72.4 0.7 copy.11
Async XLA Ops:
  0.6 1.1 %copy-start = (bf16[192,1536]{1,0:T(8,128)(2,1)S(1)}, bf16[192,1536]{1,0:T(8,128)(2,1)}, u32[]{:S(2)}) copy-start(bf16[192,1536]{1,0:T(8,128)(2,1)} %w_ref.1) | copy-start | bytes 1769476
  1.7 1.0 %copy-start.1 = (bf16[1,128,1536]{2,1,0:T(8,128)(2,1)S(1)}, bf16[1,128,1536]{2,1,0:T(8,128)(2,1)}, u32[]{:S(2)}) copy-start(bf16[1,128,1536]{2,1,0:T(8,128)(2,1)} %param.8) | copy-start | bytes 1179652
  2.7 1.0 %copy-start.2 = (bf16[1,128,1536]{2,1,0:T(8,128)(2,1)S(1)}, bf16[1,128,1536]{2,1,0:T(8,128)(2,1)}, u32[]{:S(2)}) copy-start(bf16[1,128,1536]{2,1,0:T(8,128)(2,1)} %param.9) | copy-start | bytes 1179652
  3.7 1.0 %copy-start.3 = (bf16[1,128,1536]{2,1,0:T(8,128)(2,1)S(1)}, bf16[1,128,1536]{2,1,0:T(8,128)(2,1)}, u32[]{:S(2)}) copy-start(bf16[1,128,1536]{2,1,0:T(8,128)(2,1)} %param.10) | copy-start | bytes 1179652
  4.7 0.9 %copy-start.4 = (bf16[1,128,768]{2,1,0:T(8,128)(2,1)S(1)}, bf16[1,128,768]{2,1,0:T(8,128)(2,1)}, u32[]{:S(2)}) copy-start(bf16[1,128,768]{2,1,0:T(8,128)(2,1)} %param.7) | copy-start | bytes 589828
  5.6 0.7 %copy-start.5 = (bf16[32,384]{1,0:T(8,128)(2,1)S(1)}, bf16[32,384]{1,0:T(8,128)(2,1)}, u32[]{:S(2)}) copy-start(bf16[32,384]{1,0:T(8,128)(2,1)} %ck_ref.1) | copy-start | bytes 73732
  6.4 0.7 copy-start.6

commit v2 on v1

--- a/solution.py
+++ b/solution.py
@@ -174,10 +174,10 @@
     nt, nf,
     starts_ref, q_ref, kv_ref, in_ref, cot_ref, w_ref, ck_ref,
     cg_ref, wg_ref, kg_ref,
-    kvx, qx, inx, cotx, wfull, kall, kf, seg, m1, ctx, ctx_t, res, gs, rg, kgs,
+    kvx, qx, inx, cotx, wfull, kall, kf, seg, m1, ctx, ctx_t, res, gs, rg, kgs, kgp,
     part, own, asrc, abuf, bsrc, bbuf, fsum, csrc, cbuf, gbuf,
     kgsrc, kgb, kgcs, kgc, kgds, kgd,
-    hs, hr, ws, wr, fs, fr, ks, kr, as_, ar, bs, br, cs, cr, gsn, grc, ds_, dr,
+    ls, hs, hr, ws, wr, fs, fr, ks, kr, as_, ar, bs, br, cs, cr, gsn, grc, ds_, dr,
     kbs, kbr, kcs, kcr, kds, kdr,
 ):
     nz = nt // 2
@@ -216,6 +216,20 @@
             device_id={"tm": tm, "fsdp": fsdp}, device_id_type=MESH,
         )
 
+    halo = ((kv_ref, kvx, KEY_PAD), (q_ref, qx, ROW_PAD), (in_ref, inx, ROW_PAD), (cot_ref, cotx, COT_PAD))
+    own_copies = [
+        pltpu.make_async_copy(src, dst.at[pl.ds(pad, rows)], ls.at[n])
+        for n, (src, dst, pad) in enumerate(halo)
+    ]
+    own_copies.append(
+        pltpu.make_async_copy(
+            w_ref, wfull.at[pl.ds(pl.multiple_of(f * shard, 16), shard)], ls.at[4]
+        )
+    )
+    own_copies.append(pltpu.make_async_copy(ck_ref, kall.at[f], ls.at[5]))
+    for own_copy in own_copies:
+        own_copy.start()
+
     barrier = pltpu.get_barrier_semaphore()
 
     def greet(tm, fsdp):
@@ -238,8 +252,6 @@
 
     near = jnp.minimum(t, 1) + jnp.minimum(nt - 1 - t, 1)
     pl.semaphore_wait(barrier, nf - 1 + nz - 1 + near)
-
-    halo = ((kv_ref, kvx, KEY_PAD), (q_ref, qx, ROW_PAD), (in_ref, inx, ROW_PAD), (cot_ref, cotx, COT_PAD))
 
     def up_copy(n):
         src, dst, pad = halo[n]
@@ -291,10 +303,6 @@
         for src, dst, pad in halo:
             dst[pad + rows : 2 * pad + rows] = jnp.zeros((pad, dst.shape[1]), dst.dtype)
 
-    for src, dst, pad in halo:
-        dst[pad : pad + rows] = src[...]
-    wfull[pl.ds(pl.multiple_of(f * shard, 16), shard)] = w_ref[...]
-    kall[f] = ck_ref[...]
 
     utts = starts_ref.shape[1]
 
@@ -318,6 +326,9 @@
     def _():
         for n in range(4):
             down_copy(n).wait_recv()
+
+    for own_copy in own_copies:
+        own_copy.wait()
 
     keys = 2 * LANES
     key_rows = rows + 2 * KEY_PAD
@@ -380,7 +391,9 @@
         k_copies[i - 1].wait_recv()
     for s in range(nf):
         for i in range(per_shard):
-            kf[s * per_shard + i] = kall[s, :, LANES * i : LANES * (i + 1)].astype(jnp.float32)
+            taps = kall[s, :, LANES * i : LANES * (i + 1)].astype(jnp.float32)
+            for k in range(KW):
+                kf[s * per_shard + i, k] = jnp.broadcast_to(taps[k : k + 1], (8, LANES))
     for i in range(1, nf):
         forward(i).wait_recv()
 
@@ -391,35 +404,52 @@
         for i in range(per_piece):
             res[per_piece * j + i] = out[:, LANES * i : LANES * (i + 1)]
 
+    def tiles(x):
+        return x.reshape(x.shape[0] // 8, 8, LANES)
+
     def conv_chunk(n, carry):
         columns = pl.ds(pl.multiple_of(n * LANES, LANES), LANES)
-        conv = jnp.zeros((span, LANES), jnp.float32)
-        for b in range(8):
-            shifted = res[n, pl.ds(b, span + 24), :]
-            for a in range(KW // 8):
-                k = 8 * a + b
-                conv = conv + m1[k] * (kf[n, k : k + 1, :] * shifted[8 * a : 8 * a + span])
-        sig = jax.nn.sigmoid(conv)
-        cot = cotx[:, columns].astype(jnp.float32)
-        gs[...] = cot * sig * (1.0 + conv * (1.0 - sig))
-        back = cot_ref[:, columns].astype(jnp.float32)
-        mid = slice(COT_PAD, COT_PAD + rows)
-        for b in range(8):
-            low = 8 if b == 0 else 0
-            shifted = gs[b + low : b + low + rows + 24]
-            for a in range(KW // 8):
-                o = 8 * a + b + low
-                k = KW - o
-                back = back + m1[o, mid] * (kf[n, k : k + 1, :] * shifted[8 * a : 8 * a + rows])
-        rg[:, columns] = back.astype(jnp.bfloat16)
-        grad = gs[mid]
-        for b in range(8):
-            shifted = res[n, pl.ds(COT_PAD + b, rows + 24), :]
-            for a in range(KW // 8):
-                k = 8 * a + b
-                prod = m1[k, mid] * grad * shifted[8 * a : 8 * a + rows]
-                prod = jnp.sum(prod.reshape(rows // 8, 8, LANES), axis=0)
-                kgs[n, k : k + 1, :] = jnp.sum(prod, axis=0, keepdims=True)
+        part_rows = span // 2
+        for h in range(2):
+            lead = part_rows * h
+            conv = jnp.zeros((part_rows // 8, 8, LANES), jnp.float32)
+            for b in range(8):
+                shifted = tiles(res[n, pl.ds(lead + b, part_rows + 24), :])
+                for a in range(KW // 8):
+                    k = 8 * a + b
+                    mask = tiles(m1[k, lead : lead + part_rows])
+                    conv = conv + mask * (kf[n, k][None] * shifted[a : a + part_rows // 8])
+            conv = conv.reshape(part_rows, LANES)
+            sig = jax.nn.sigmoid(conv)
+            cot = cotx[lead : lead + part_rows, columns].astype(jnp.float32)
+            gs[lead : lead + part_rows] = cot * sig * (1.0 + conv * (1.0 - sig))
+        part_rows = rows // 2
+        for h in range(2):
+            lead = part_rows * h
+            mid = slice(COT_PAD + lead, COT_PAD + lead + part_rows)
+            back = tiles(cotx[mid, columns].astype(jnp.float32))
+            for b in range(8):
+                low = 8 if b == 0 else 0
+                shifted = tiles(gs[lead + b + low : lead + b + low + part_rows + 24])
+                for a in range(KW // 8):
+                    o = 8 * a + b + low
+                    mask = tiles(m1[o, mid])
+                    back = back + mask * (kf[n, KW - o][None] * shifted[a : a + part_rows // 8])
+            rg[lead : lead + part_rows, columns] = back.reshape(part_rows, LANES).astype(jnp.bfloat16)
+        for h in range(2):
+            lead = part_rows * h
+            mid = slice(COT_PAD + lead, COT_PAD + lead + part_rows)
+            grad = tiles(gs[mid])
+            for b in range(8):
+                shifted = tiles(res[n, pl.ds(COT_PAD + lead + b, part_rows + 24), :])
+                for a in range(KW // 8):
+                    k = 8 * a + b
+                    mask = tiles(m1[k, mid])
+                    prod = jnp.sum(mask * grad * shifted[a : a + part_rows // 8], axis=0)
+                    if h == 0:
+                        kgp[k] = prod
+                    else:
+                        kgs[n, k : k + 1, :] = jnp.sum(prod + kgp[k], axis=0, keepdims=True)
         return carry
 
     def a_copy(j):
@@ -607,7 +637,7 @@
         ((span, width), bf16),
         ((head_width, width), bf16),
         ((nf, KW, width // nf), bf16),
-        ((chunks, KW, LANES), f32),
+        ((chunks, KW, 8, LANES), f32),
         ((ext, LANES), f32),
         ((KW + 1, span, LANES), f32),
         ((ext, head_width), bf16),
@@ -616,6 +646,7 @@
         ((span, LANES), f32),
         ((rows, width), bf16),
         ((chunks, KW, LANES), f32),
+        ((KW, 8, LANES), f32),
         ((head_width, chunk_w), f32),
         ((nz, nf, half, chunk_w), f32),
         ((nz, nf, half, chunk_w), bf16),
@@ -634,7 +665,7 @@
         ((per_shard, KW, LANES), bf16),
     ]
     sems = [
-        (2, 4), (2, 4), (nf,), (nf,), (nf,), (nf,), (nf,), (nf,), (nz,), (nz,), (nz, nf), (nz, nf),
+        (6,), (2, 4), (2, 4), (nf,), (nf,), (nf,), (nf,), (nf,), (nf,), (nz,), (nz,), (nz, nf), (nz, nf),
         (nz,), (nz,), (nz,), (nz,), (nz,), (nz,), (nf,), (nf,), (nz,), (nz,),
     ]
     context_grad, weight_grad, kernel_grad = pl.pallas_call(
@@ -644,7 +675,7 @@
             jax.ShapeDtypeStruct((shard, width), bf16),
             jax.ShapeDtypeStruct((KW, width // nf), f32),
         ),
-        in_specs=[pl.BlockSpec(memory_space=pltpu.SMEM)] + [vmem] * 6,
+        in_specs=[pl.BlockSpec(memory_space=pltpu.SMEM)] + [pl.BlockSpec(memory_space=pltpu.HBM)] * 6,
         out_specs=(vmem, vmem, vmem),
         scratch_shapes=[pltpu.VMEM(*s) for s in scratch]
         + [dma(s) for s in sems]

time: 73.5 us -> 73.7 us (level)
  no operation moved by 1% of the time
where the time goes in v2:
time: 73.7 us; the launch traced here: 73.3 us
  Pallas kernels  63.8 us (87%)
  local copies, waits for them, and re-layouts  7.04 us (10%)
  other arithmetic  1.77 us (2%)
    pallas_call x1, Pallas kernels, fused(): pl.pallas_call(functools.partial(block_kernel, nt, nf), out_shape=(jax.Sh...  63.8 us
    unnamed x15, local copies, waits for them, and re-layouts  7.04 us

profile of v2, /device:TPU:1, one launch (start us, length us, event | category | flops | bytes accessed | tf_op | source)
XLA Modules:
  0.0 73.3 jit_solution(4629782545575893683)
XLA Ops:
  0.6 0.0 copy-start
  0.6 1.1 %copy-done = bf16[192,1536]{1,0:T(8,128)(2,1)S(1)} copy-done((bf16[192,1536]{1,0:T(8,128)(2,1)S(1)}, bf16[192,1536]{1,0:T(8,128)(2,1)}, u32[]{:S(2)}) %copy-start) | copy-done | bytes 589848
  1.7 0.0 copy-start.1
  1.7 1.0 %copy-done.1 = bf16[1,128,1536]{2,1,0:T(8,128)(2,1)S(1)} copy-done((bf16[1,128,1536]{2,1,0:T(8,128)(2,1)S(1)}, bf16[1,128,1536]{2,1,0:T(8,128)(2,1)}, u32[]{:S(2)}) %copy-start.1) | copy-done | bytes 393240
  2.7 0.0 copy-start.2
  2.7 1.0 %copy-done.2 = bf16[1,128,1536]{2,1,0:T(8,128)(2,1)S(1)} copy-done((bf16[1,128,1536]{2,1,0:T(8,128)(2,1)S(1)}, bf16[1,128,1536]{2,1,0:T(8,128)(2,1)}, u32[]{:S(2)}) %copy-start.2) | copy-done | bytes 393240
  3.7 0.0 copy-start.3
  3.7 1.0 %copy-done.3 = bf16[1,128,1536]{2,1,0:T(8,128)(2,1)S(1)} copy-done((bf16[1,128,1536]{2,1,0:T(8,128)(2,1)S(1)}, bf16[1,128,1536]{2,1,0:T(8,128)(2,1)}, u32[]{:S(2)}) %copy-start.3) | copy-done | bytes 393240
  4.7 0.0 copy-start.4
  4.7 0.9 %copy-done.4 = bf16[1,128,768]{2,1,0:T(8,128)(2,1)S(1)} copy-done((bf16[1,128,768]{2,1,0:T(8,128)(2,1)S(1)}, bf16[1,128,768]{2,1,0:T(8,128)(2,1)}, u32[]{:S(2)}) %copy-start.4) | copy-done | bytes 196632
  5.6 0.0 copy-start.5
  5.6 0.7 %copy-done.5 = bf16[32,384]{1,0:T(8,128)(2,1)S(1)} copy-done((bf16[32,384]{1,0:T(8,128)(2,1)S(1)}, bf16[32,384]{1,0:T(8,128)(2,1)}, u32[]{:S(2)}) %copy-start.5) | copy-done | bytes 24600
  6.4 0.0 copy-start.6
  6.4 0.7 copy-done.6
  7.0 63.8 %shard_map.94 = (bf16[128,768]{1,0:T(8,128)(2,1)S(1)}, bf16[192,1536]{1,0:T(8,128)(2,1)S(1)}, f32[32,384]{1,0:T(8,128)S(1)}) custom-call(s32[1,16]{1,0:T(1,128)S(1)} %copy-done.6, bf16[128,768]{1,0:T(8,128)(2,1)S(1)} %bitcast.8, bf16[128,1536]{1,0:T(8,128)(2,1)S(1)} %bitcast.5, bf16[128,1536]{1,0:T(8,128)(2,1)S(1)} %bitcast.6, ...), custom_call_target="tpu_custom_call" | custom-call | tf_op jit(solution)/shard_map/pallas_call | solution.py:671
  70.8 0.6 broadcast_multiply_fusion
  71.5 1.1 %convert_multiply_fusion = f32[192,1536]{1,0:T(8,128)} fusion(bf16[192,1536]{1,0:T(8,128)(2,1)S(1)} %get-tuple-element.7), kind=kLoop, calls=%fused_computation | loop fusion | flops 589824 | bytes 1769472 | tf_op jit(solution)/shard_map/mul | solution.py:690
  72.6 0.7 copy.11
Async XLA Ops:
  0.6 1.1 %copy-start = (bf16[192,1536]{1,0:T(8,128)(2,1)S(1)}, bf16[192,1536]{1,0:T(8,128)(2,1)}, u32[]{:S(2)}) copy-start(bf16[192,1536]{1,0:T(8,128)(2,1)} %w_ref.1) | copy-start | bytes 1769476
  1.7 1.0 %copy-start.1 = (bf16[1,128,1536]{2,1,0:T(8,128)(2,1)S(1)}, bf16[1,128,1536]{2,1,0:T(8,128)(2,1)}, u32[]{:S(2)}) copy-start(bf16[1,128,1536]{2,1,0:T(8,128)(2,1)} %param.8) | copy-start | bytes 1179652
  2.7 1.0 %copy-start.2 = (bf16[1,128,1536]{2,1,0:T(8,128)(2,1)S(1)}, bf16[1,128,1536]{2,1,0:T(8,128)(2,1)}, u32[]{:S(2)}) copy-start(bf16[1,128,1536]{2,1,0:T(8,128)(2,1)} %param.9) | copy-start | bytes 1179652
  3.7 1.0 %copy-start.3 = (bf16[1,128,1536]{2,1,0:T(8,128)(2,1)S(1)}, bf16[1,128,1536]{2,1,0:T(8,128)(2,1)}, u32[]{:S(2)}) copy-start(bf16[1,128,1536]{2,1,0:T(8,128)(2,1)} %param.10) | copy-start | bytes 1179652
  4.7 0.9 %copy-start.4 = (bf16[1,128,768]{2,1,0:T(8,128)(2,1)S(1)}, bf16[1,128,768]{2,1,0:T(8,128)(2,1)}, u32[]{:S(2)}) copy-start(bf16[1,128,768]{2,1,0:T(8,128)(2,1)} %param.7) | copy-start | bytes 589828
  5.6 0.7 %copy-start.5 = (bf16[32,384]{1,0:T(8,128)(2,1)S(1)}, bf16[32,384]{1,0:T(8,128)(2,1)}, u32[]{:S(2)}) copy-start(bf16[32,384]{1,0:T(8,128)(2,1)} %ck_ref.1) | copy-start | bytes 73732
  6.4 0.7 copy-start.6

commit v3 on v2

--- a/solution.py
+++ b/solution.py
@@ -158,6 +158,7 @@
 KEY_PAD = 96
 ROW_PAD = 32
 COT_PAD = 16
+GROUP = 32
 BLOCK = 64
 LANES = 128
 
@@ -174,7 +175,7 @@
     nt, nf,
     starts_ref, q_ref, kv_ref, in_ref, cot_ref, w_ref, ck_ref,
     cg_ref, wg_ref, kg_ref,
-    kvx, qx, inx, cotx, wfull, kall, kf, seg, m1, ctx, ctx_t, res, gs, rg, kgs, kgp,
+    kvx, qx, inx, cotx, wfull, kall, kf, seg, m1, ctx, ctx_t, res, gs, rg, kgs, kgp, ms,
     part, own, asrc, abuf, bsrc, bbuf, fsum, csrc, cbuf, gbuf,
     kgsrc, kgb, kgcs, kgc, kgds, kgd,
     ls, hs, hr, ws, wr, fs, fr, ks, kr, as_, ar, bs, br, cs, cr, gsn, grc, ds_, dr,
@@ -278,20 +279,23 @@
     def rows_of(owner, core):
         return pl.ds(pl.multiple_of(owner * shard + core * half, 16), half)
 
-    w_copies = [
-        copy(
-            w_ref.at[pl.ds(pl.multiple_of(c * half, 16), half)], wfull.at[rows_of(f, c)],
-            ws.at[i], wr.at[i], t, other_f(i),
-        )
-        for i in range(1, nf)
-    ]
+    def cols(j):
+        return pl.ds(chunk_w * j, chunk_w)
+
+    def w_copy(j, i):
+        return copy(
+            w_ref.at[pl.ds(pl.multiple_of(c * half, 16), half), cols(j)],
+            wfull.at[rows_of(f, c), cols(j)], ws.at[j, i], wr.at[j, i], t, other_f(i),
+        )
+
     k_copies = [
         copy(ck_ref, kall.at[f], ks.at[i], kr.at[i], t, other_f(i)) for i in range(1, nf)
     ]
-    for w_copy in w_copies:
-        w_copy.start()
     for k_copy in k_copies:
         k_copy.start()
+    for j in range(nz):
+        for i in range(1, nf):
+            w_copy(j, i).start()
 
     @pl.when(t == 0)
     def _():
@@ -380,13 +384,16 @@
             )
     ctx_t[...] = ctx[ROW_PAD : ROW_PAD + rows].astype(jnp.float32).T.astype(jnp.bfloat16)
 
-    def forward(i):
-        piece = wfull.at[rows_of(from_f(i), c)]
-        return copy(piece, piece, fs.at[i], fr.at[i], sib, f)
-
-    for i in range(1, nf):
-        w_copies[i - 1].wait_recv()
-        forward(i).start()
+    def forward(j, i):
+        piece = wfull.at[rows_of(from_f(i), c), cols(j)]
+        return copy(piece, piece, fs.at[j, i], fr.at[j, i], sib, f)
+
+    def pass_on(j):
+        for i in range(1, nf):
+            w_copy(j, i).wait_recv()
+            forward(j, i).start()
+
+    pass_on(0)
     for i in range(1, nf):
         k_copies[i - 1].wait_recv()
     for s in range(nf):
@@ -394,10 +401,9 @@
             taps = kall[s, :, LANES * i : LANES * (i + 1)].astype(jnp.float32)
             for k in range(KW):
                 kf[s * per_shard + i, k] = jnp.broadcast_to(taps[k : k + 1], (8, LANES))
-    for i in range(1, nf):
-        forward(i).wait_recv()
-
-    for j in range(nz):
+    def project(j):
+        for i in range(1, nf):
+            forward(j, i).wait_recv()
         columns = slice(chunk_w * j, chunk_w * (j + 1))
         out = inx[:, columns].astype(jnp.float32) + dot(ctx[...], wfull[:, columns])
         out = out.astype(jnp.bfloat16).astype(jnp.float32)
@@ -405,52 +411,56 @@
             res[per_piece * j + i] = out[:, LANES * i : LANES * (i + 1)]
 
     def tiles(x):
-        return x.reshape(x.shape[0] // 8, 8, LANES)
-
-    def conv_chunk(n, carry):
-        columns = pl.ds(pl.multiple_of(n * LANES, LANES), LANES)
-        part_rows = span // 2
-        for h in range(2):
-            lead = part_rows * h
-            conv = jnp.zeros((part_rows // 8, 8, LANES), jnp.float32)
+        return x.reshape(x.shape[:-2] + (x.shape[-2] // 8, 8, LANES))
+
+    def conv_group(j):
+        lanes = slice(per_piece * j, per_piece * (j + 1))
+
+        def cot_rows(lead):
+            return jnp.stack(
+                [
+                    cotx[lead : lead + GROUP, LANES * n : LANES * (n + 1)].astype(jnp.float32)
+                    for n in range(per_piece * j, per_piece * (j + 1))
+                ]
+            )
+
+        for lead in range(0, span, GROUP):
+            conv = jnp.zeros((per_piece, GROUP // 8, 8, LANES), jnp.float32)
             for b in range(8):
-                shifted = tiles(res[n, pl.ds(lead + b, part_rows + 24), :])
+                shifted = tiles(res[lanes, lead + b : lead + b + GROUP + 24, :])
                 for a in range(KW // 8):
                     k = 8 * a + b
-                    mask = tiles(m1[k, lead : lead + part_rows])
-                    conv = conv + mask * (kf[n, k][None] * shifted[a : a + part_rows // 8])
-            conv = conv.reshape(part_rows, LANES)
+                    mask = tiles(m1[k, lead : lead + GROUP])
+                    kept = mask[None] * shifted[:, a : a + GROUP // 8]
+                    ms[k, :, lead : lead + GROUP] = kept.reshape(per_piece, GROUP, LANES)
+                    conv = conv + kf[lanes, k][:, None] * kept
+            conv = conv.reshape(per_piece, GROUP, LANES)
             sig = jax.nn.sigmoid(conv)
-            cot = cotx[lead : lead + part_rows, columns].astype(jnp.float32)
-            gs[lead : lead + part_rows] = cot * sig * (1.0 + conv * (1.0 - sig))
-        part_rows = rows // 2
-        for h in range(2):
-            lead = part_rows * h
-            mid = slice(COT_PAD + lead, COT_PAD + lead + part_rows)
-            back = tiles(cotx[mid, columns].astype(jnp.float32))
+            gs[:, lead : lead + GROUP] = cot_rows(lead) * sig * (1.0 + conv * (1.0 - sig))
+        for lead in range(0, rows, GROUP):
+            mid = slice(COT_PAD + lead, COT_PAD + lead + GROUP)
+            back = tiles(cot_rows(COT_PAD + lead))
             for b in range(8):
                 low = 8 if b == 0 else 0
-                shifted = tiles(gs[lead + b + low : lead + b + low + part_rows + 24])
+                shifted = tiles(gs[:, lead + b + low : lead + b + low + GROUP + 24])
                 for a in range(KW // 8):
                     o = 8 * a + b + low
                     mask = tiles(m1[o, mid])
-                    back = back + mask * (kf[n, KW - o][None] * shifted[a : a + part_rows // 8])
-            rg[lead : lead + part_rows, columns] = back.reshape(part_rows, LANES).astype(jnp.bfloat16)
-        for h in range(2):
-            lead = part_rows * h
-            mid = slice(COT_PAD + lead, COT_PAD + lead + part_rows)
-            grad = tiles(gs[mid])
-            for b in range(8):
-                shifted = tiles(res[n, pl.ds(COT_PAD + lead + b, part_rows + 24), :])
-                for a in range(KW // 8):
-                    k = 8 * a + b
-                    mask = tiles(m1[k, mid])
-                    prod = jnp.sum(mask * grad * shifted[a : a + part_rows // 8], axis=0)
-                    if h == 0:
-                        kgp[k] = prod
-                    else:
-                        kgs[n, k : k + 1, :] = jnp.sum(prod + kgp[k], axis=0, keepdims=True)
-        return carry
+                    back = back + mask[None] * (
+                        kf[lanes, KW - o][:, None] * shifted[:, a : a + GROUP // 8]
+                    )
+            back = back.reshape(per_piece, GROUP, LANES).astype(jnp.bfloat16)
+            for i in range(per_piece):
+                n = per_piece * j + i
+                rg[lead : lead + GROUP, LANES * n : LANES * (n + 1)] = back[i]
+        for lead in range(0, rows, 2 * GROUP):
+            mid = slice(COT_PAD + lead, COT_PAD + lead + 2 * GROUP)
+            grad = tiles(gs[:, mid])
+            for k in range(KW):
+                prod = jnp.sum(grad * tiles(ms[k, :, mid]), axis=1)
+                kgp[k] = prod if lead == 0 else prod + kgp[k]
+        for i in range(per_piece):
+            kgs[per_piece * j + i] = jnp.sum(kgp[:, i], axis=1)
 
     def a_copy(j):
         return copy(asrc.at[j], abuf.at[j], as_.at[j], ar.at[j], sib, f)
@@ -460,8 +470,44 @@
             bsrc.at[j, other_f(i)], bbuf.at[j, i], bs.at[j, i], br.at[j, i], t, other_f(i)
         )
 
+    owners = sorted(range(nz), key=lambda s: -abs(2 * s - nz + 1))
+
     def c_copy(j):
-        return copy(csrc.at[j], cbuf.at[z], cs.at[j], cr.at[z], 2 * j + c, f)
+        return copy(csrc.at[j], cbuf.at[z], cs.at[j], cr.at[z], 2 * owners[j] + c, f)
+
+    def c_from(i):
+        s = other_z(i)
+        return copy(csrc.at[0], cbuf.at[s], cs.at[0], cr.at[s], 2 * s + c, f)
+
+    def g_copy(j, i):
+        piece = gbuf.at[c, j]
+        return copy(piece, piece, gsn.at[i], grc.at[j], 2 * other_z(i) + c, f)
+
+    def d_copy(j):
+        piece = gbuf.at[c, j]
+        return copy(piece, piece, ds_.at[j], dr.at[j], sib, f)
+
+    def d_from(j):
+        piece = gbuf.at[1 - c, j]
+        return copy(piece, piece, ds_.at[j], dr.at[j], sib, f)
+
+    def finish_c(j):
+        @pl.when(z == owners[j])
+        def _():
+            final = fsum[...]
+            for i in range(1, nz):
+                c_from(i).wait_recv()
+                final = final + cbuf[other_z(i)].astype(jnp.float32)
+            gbuf[c, j] = final.astype(jnp.bfloat16)
+            for i in range(1, nz):
+                g_copy(j, i).start()
+            d_copy(j).start()
+
+    def take(j):
+        @pl.when(z != owners[j])
+        def _():
+            g_copy(j, 1).wait_recv()
+            d_copy(j).start()
 
     def finish_a(j):
         a_copy(j).wait_recv()
@@ -476,17 +522,20 @@
             b_copy(j, i).wait_recv()
             acc = acc + bbuf[j, i].astype(jnp.float32)
 
-        @pl.when(z == j)
+        @pl.when(z == owners[j])
         def _():
             fsum[...] = acc
 
-        @pl.when(z != j)
+        @pl.when(z != owners[j])
         def _():
             csrc[j] = acc.astype(jnp.bfloat16)
             c_copy(j).start()
 
     for j in range(nz):
-        lax.fori_loop(per_piece * j, per_piece * (j + 1), conv_chunk, 0)
+        project(j)
+        if j + 1 < nz:
+            pass_on(j + 1)
+        conv_group(j)
         part[...] = dot(ctx_t[...], rg[:, chunk_w * j : chunk_w * (j + 1)])
         for s in range(nf):
             own[j, s] = part[rows_of(s, c)]
@@ -496,6 +545,8 @@
             finish_a(j - 1)
         if j >= 2:
             finish_b(j - 2)
+        if j >= 3:
+            finish_c(j - 3)
 
     def kb_copy(i):
         return copy(kgsrc.at[other_f(i)], kgb.at[i], kbs.at[i], kbr.at[i], t, other_f(i))
@@ -508,6 +559,8 @@
     finish_a(nz - 1)
     if nz >= 2:
         finish_b(nz - 2)
+    if nz >= 3:
+        finish_c(nz - 3)
     cg_ref[...] = dot_t(rg[...], wfull[...]).astype(jnp.bfloat16)
 
     kg_sum = kgs[pl.ds(f * per_shard, per_shard)]
@@ -528,36 +581,11 @@
     kgc[z] = kgcs[...]
     finish_b(nz - 1)
 
-    def c_from(i):
-        s = other_z(i)
-        return copy(csrc.at[0], cbuf.at[s], cs.at[0], cr.at[s], 2 * s + c, f)
-
-    final = fsum[...]
-    for i in range(1, nz):
-        c_from(i).wait_recv()
-        final = final + cbuf[other_z(i)].astype(jnp.float32)
-    gbuf[c, z] = final.astype(jnp.bfloat16)
-
-    def g_copy(i):
-        piece = gbuf.at[c, z]
-        return copy(piece, piece, gsn.at[i], grc.at[z], 2 * other_z(i) + c, f)
-
-    def g_from(i):
-        s = other_z(i)
-        piece = gbuf.at[c, s]
-        return copy(piece, piece, gsn.at[i], grc.at[s], 2 * s + c, f)
-
-    def d_copy(s):
-        piece = gbuf.at[c, s]
-        return copy(piece, piece, ds_.at[s], dr.at[s], sib, f)
-
-    def d_from(s):
-        piece = gbuf.at[1 - c, s]
-        return copy(piece, piece, ds_.at[s], dr.at[s], sib, f)
-
-    for i in range(1, nz):
-        g_copy(i).start()
-    d_copy(z).start()
+    if nz >= 2:
+        finish_c(nz - 2)
+    for j in range(nz - 2):
+        take(j)
+    finish_c(nz - 1)
 
     for i in range(1, nz):
         kc_from(i).wait_recv()
@@ -568,9 +596,8 @@
     kd_copy = copy(kgds, kgd, kds, kdr, sib, f)
     kd_copy.start()
 
-    for i in range(1, nz):
-        g_from(i).wait_recv()
-        d_copy(other_z(i)).start()
+    for j in range(max(nz - 2, 0), nz):
+        take(j)
     kd_copy.wait_recv()
     kg_all = kgds[...].astype(jnp.float32) + kgd[...].astype(jnp.float32)
     for i in range(per_shard):
@@ -579,9 +606,8 @@
     theirs = pl.ds(pl.multiple_of((1 - c) * half, 16), half)
     for s in range(nz):
         wg_ref[mine, chunk_w * s : chunk_w * (s + 1)] = gbuf[c, s]
-    for i in range(nz):
-        d_from(other_z(i)).wait_recv()
     for s in range(nz):
+        d_from(s).wait_recv()
         wg_ref[theirs, chunk_w * s : chunk_w * (s + 1)] = gbuf[1 - c, s]
 
     @pl.when(t < nt - 1)
@@ -595,24 +621,24 @@
             down_copy(n).wait_send()
 
     for i in range(1, nf):
-        w_copies[i - 1].wait_send()
         k_copies[i - 1].wait_send()
-        forward(i).wait_send()
         kb_copy(i).wait_send()
     for j in range(nz):
         a_copy(j).wait_send()
         for i in range(1, nf):
+            w_copy(j, i).wait_send()
+            forward(j, i).wait_send()
             b_copy(j, i).wait_send()
 
-        @pl.when(z != j)
+        @pl.when(z != owners[j])
         def _():
             c_copy(j).wait_send()
 
     for i in range(1, nz):
         kc_copy(i).wait_send()
-        g_copy(i).wait_send()
-    for i in range(nz):
-        d_copy(other_z(i)).wait_send()
+        g_copy(0, i).wait_send()
+    for j in range(nz):
+        d_copy(j).wait_send()
     kd_copy.wait_send()
 
 
@@ -625,6 +651,7 @@
     chunks = width // LANES
     per_shard = chunks // nf
     chunk_w = width // nz
+    per_piece = chunks // nz
     ext = rows + 2 * ROW_PAD
     span = rows + 2 * COT_PAD
     bf16, f32 = jnp.bfloat16, jnp.float32
@@ -643,10 +670,11 @@
         ((ext, head_width), bf16),
         ((head_width, rows), bf16),
         ((chunks, ext, LANES), f32),
-        ((span, LANES), f32),
+        ((per_piece, span, LANES), f32),
         ((rows, width), bf16),
         ((chunks, KW, LANES), f32),
-        ((KW, 8, LANES), f32),
+        ((KW, per_piece, 8, LANES), f32),
+        ((KW, per_piece, span, LANES), f32),
         ((head_width, chunk_w), f32),
         ((nz, nf, half, chunk_w), f32),
         ((nz, nf, half, chunk_w), bf16),
@@ -665,7 +693,7 @@
         ((per_shard, KW, LANES), bf16),
     ]
     sems = [
-        (6,), (2, 4), (2, 4), (nf,), (nf,), (nf,), (nf,), (nf,), (nf,), (nz,), (nz,), (nz, nf), (nz, nf),
+        (6,), (2, 4), (2, 4), (nz, nf), (nz, nf), (nz, nf), (nz, nf), (nf,), (nf,), (nz,), (nz,), (nz, nf), (nz, nf),
         (nz,), (nz,), (nz,), (nz,), (nz,), (nz,), (nf,), (nf,), (nz,), (nz,),
     ]
     context_grad, weight_grad, kernel_grad = pl.pallas_call(
@@ -681,7 +709,7 @@
         + [dma(s) for s in sems]
         + [dma, dma],
         compiler_params=pltpu.CompilerParams(
-            collective_id=0, has_side_effects=True, vmem_limit_bytes=48 * 1024 * 1024
+            collective_id=0, has_side_effects=True, vmem_limit_bytes=60 * 1024 * 1024
         ),
     )(utt_starts, queries[0], keys_values[0], inputs[0], cotangent[0], out_weight, conv_kernel)
     grad_scale = 1.0 / math.sqrt(nf * queries.shape[0] * nt * rows)

time: 73.7 us -> 63.6 us (0.86)
  local copies, waits for them, and re-layouts: 7.04 us -> 0.68 us
  Pallas kernels: 63.8 us -> 58.4 us
  other arithmetic: 1.77 us -> 3.67 us
    unnamed x15 -> x3, local copies, waits for them, and re-layouts: 7.04 us -> 0.68 us
    pallas_call x1, Pallas kernels: 63.8 us -> 58.4 us  [fused(): pl.pallas_call(functools.partial(block_kernel, nt, nf), out_shape=(jax.Sh...]
    mul x1, other arithmetic: 1.15 us -> 2.21 us  [fused(): weight_grad.astype(jnp.float32) * grad_scale]
    mul x1, other arithmetic: 0.63 us -> 1.46 us  [fused(): kernel_grad * grad_scale]
where the time goes in v3:
time: 63.6 us; the launch traced here: 63.4 us
  Pallas kernels  58.4 us (92%)
  other arithmetic  3.67 us (6%)
  local copies, waits for them, and re-layouts  0.68 us (1%)
  between operations  0.65 us (1%)
    pallas_call x1, Pallas kernels, fused(): pl.pallas_call(functools.partial(block_kernel, nt, nf), out_shape=(jax.Sh...  58.4 us
    mul x1, other arithmetic, fused(): weight_grad.astype(jnp.float32) * grad_scale  2.21 us
    mul x1, other arithmetic, fused(): kernel_grad * grad_scale  1.46 us

profile of v3, /device:TPU:1, one launch (start us, length us, event | category | flops | bytes accessed | tf_op | source)
XLA Modules:
  0.0 63.4 jit_solution(16134985949195590386)
XLA Ops:
  0.6 58.4 %shard_map.94 = (bf16[128,768]{1,0:T(8,128)(2,1)}, bf16[192,1536]{1,0:T(8,128)(2,1)}, f32[32,384]{1,0:T(8,128)}) custom-call(s32[1,16]{1,0:T(1,128)} %starts_ref.1, bf16[128,768]{1,0:T(8,128)(2,1)} %bitcast.8, bf16[128,1536]{1,0:T(8,128)(2,1)} %bitcast.5, bf16[128,1536]{1,0:T(8,128)(2,1)} %bitcast.6, bf16[128,1536]{1,0:T(8,128)(2,1)} %bitcast.7, ...), custom_call_target="tpu_custom_call" | custom-call | tf_op jit(solution)/shard_map/pallas_call | solution.py:699
  59.1 0.0 copy-start
  59.1 1.5 %broadcast_multiply_fusion = f32[32,384]{1,0:T(8,128)} fusion(f32[32,384]{1,0:T(8,128)} %get-tuple-element.8), kind=kLoop, calls=%fused_computation.1 | loop fusion | flops 12288 | bytes 98304 | tf_op jit(solution)/shard_map/mul | solution.py:719
  60.6 2.2 %convert_multiply_fusion = f32[192,1536]{1,0:T(8,128)} fusion(bf16[192,1536]{1,0:T(8,128)(2,1)} %get-tuple-element.7), kind=kLoop, calls=%fused_computation | loop fusion | flops 589824 | bytes 1769472 | tf_op jit(solution)/shard_map/mul | solution.py:718
  62.8 0.0 copy-done
  62.8 0.7 %copy.11 = bf16[1,128,768]{2,1,0:T(8,128)(2,1)} copy(bf16[1,128,768]{2,1,0:T(8,128)(2,1)S(1)} %bitcast.9) | data formatting | bytes 393216
Async XLA Ops:
  59.1 3.7 %copy-start = (bf16[128,768]{1,0:T(8,128)(2,1)S(1)}, bf16[128,768]{1,0:T(8,128)(2,1)}, u32[]{:S(2)}) copy-start(bf16[128,768]{1,0:T(8,128)(2,1)} %get-tuple-element.6) | copy-start | bytes 589828

commit v4 on v3

--- a/solution.py
+++ b/solution.py
@@ -176,7 +176,7 @@
     starts_ref, q_ref, kv_ref, in_ref, cot_ref, w_ref, ck_ref,
     cg_ref, wg_ref, kg_ref,
     kvx, qx, inx, cotx, wfull, kall, kf, seg, m1, ctx, ctx_t, res, gs, rg, kgs, kgp, ms,
-    part, own, asrc, abuf, bsrc, bbuf, fsum, csrc, cbuf, gbuf,
+    part, asrc, abuf, bsrc, bbuf, fsum, csrc, cbuf, gbuf,
     kgsrc, kgb, kgcs, kgc, kgds, kgd,
     ls, hs, hr, ws, wr, fs, fr, ks, kr, as_, ar, bs, br, cs, cr, gsn, grc, ds_, dr,
     kbs, kbr, kcs, kcr, kds, kdr,
@@ -201,6 +201,7 @@
     span = rows + 2 * COT_PAD
     first = t * rows
     total = nt * rows
+    grad_scale = 1.0 / math.sqrt(nf * total)
 
     def other_f(i):
         return lax.rem(f + i, nf)
@@ -321,18 +322,30 @@
     for k in range(KW + 1):
         m1[k] = jnp.where(seg[k : k + span] == seg[COT_PAD : COT_PAD + span], 1.0, 0.0)
 
-    @pl.when(t > 0)
-    def _():
-        for n in range(4):
-            up_copy(n).wait_recv()
-
-    @pl.when(t < nt - 1)
-    def _():
-        for n in range(4):
-            down_copy(n).wait_recv()
-
+    def halo_arrived(arrays):
+        @pl.when(t > 0)
+        def _():
+            for n in arrays:
+                up_copy(n).wait_recv()
+
+        @pl.when(t < nt - 1)
+        def _():
+            for n in arrays:
+                down_copy(n).wait_recv()
+
+    def forward(j, i):
+        piece = wfull.at[rows_of(from_f(i), c), cols(j)]
+        return copy(piece, piece, fs.at[j, i], fr.at[j, i], sib, f)
+
+    def pass_on(j):
+        for i in range(1, nf):
+            w_copy(j, i).wait_recv()
+            forward(j, i).start()
+
+    halo_arrived((0, 1))
     for own_copy in own_copies:
         own_copy.wait()
+    pass_on(0)
 
     keys = 2 * LANES
     key_rows = rows + 2 * KEY_PAD
@@ -384,16 +397,8 @@
             )
     ctx_t[...] = ctx[ROW_PAD : ROW_PAD + rows].astype(jnp.float32).T.astype(jnp.bfloat16)
 
-    def forward(j, i):
-        piece = wfull.at[rows_of(from_f(i), c), cols(j)]
-        return copy(piece, piece, fs.at[j, i], fr.at[j, i], sib, f)
-
-    def pass_on(j):
-        for i in range(1, nf):
-            w_copy(j, i).wait_recv()
-            forward(j, i).start()
-
-    pass_on(0)
+    pass_on(1)
+    halo_arrived((2, 3))
     for i in range(1, nf):
         k_copies[i - 1].wait_recv()
     for s in range(nf):
@@ -437,6 +442,8 @@
             conv = conv.reshape(per_piece, GROUP, LANES)
             sig = jax.nn.sigmoid(conv)
             gs[:, lead : lead + GROUP] = cot_rows(lead) * sig * (1.0 + conv * (1.0 - sig))
+        if j >= 1:
+            finish_a(j - 1)
         for lead in range(0, rows, GROUP):
             mid = slice(COT_PAD + lead, COT_PAD + lead + GROUP)
             back = tiles(cot_rows(COT_PAD + lead))
@@ -512,12 +519,12 @@
     def finish_a(j):
         a_copy(j).wait_recv()
         for s in range(nf):
-            bsrc[j, s] = (own[j, s] + abuf[j, s].astype(jnp.float32)).astype(jnp.bfloat16)
+            bsrc[j, s] = (part[j, rows_of(s, c)] + abuf[j, s].astype(jnp.float32)).astype(jnp.bfloat16)
         for i in range(1, nf):
             b_copy(j, i).start()
 
     def finish_b(j):
-        acc = own[j, f] + abuf[j, f].astype(jnp.float32)
+        acc = part[j, rows_of(f, c)] + abuf[j, f].astype(jnp.float32)
         for i in range(1, nf):
             b_copy(j, i).wait_recv()
             acc = acc + bbuf[j, i].astype(jnp.float32)
@@ -533,16 +540,13 @@
 
     for j in range(nz):
         project(j)
-        if j + 1 < nz:
-            pass_on(j + 1)
+        if j + 2 < nz:
+            pass_on(j + 2)
         conv_group(j)
-        part[...] = dot(ctx_t[...], rg[:, chunk_w * j : chunk_w * (j + 1)])
+        part[j] = dot(ctx_t[...], rg[:, chunk_w * j : chunk_w * (j + 1)])
         for s in range(nf):
-            own[j, s] = part[rows_of(s, c)]
-            asrc[j, s] = part[rows_of(s, 1 - c)].astype(jnp.bfloat16)
+            asrc[j, s] = part[j, rows_of(s, 1 - c)].astype(jnp.bfloat16)
         a_copy(j).start()
-        if j >= 1:
-            finish_a(j - 1)
         if j >= 2:
             finish_b(j - 2)
         if j >= 3:
@@ -601,14 +605,14 @@
     kd_copy.wait_recv()
     kg_all = kgds[...].astype(jnp.float32) + kgd[...].astype(jnp.float32)
     for i in range(per_shard):
-        kg_ref[:, LANES * i : LANES * (i + 1)] = kg_all[i]
+        kg_ref[:, LANES * i : LANES * (i + 1)] = kg_all[i] * grad_scale
     mine = pl.ds(pl.multiple_of(c * half, 16), half)
     theirs = pl.ds(pl.multiple_of((1 - c) * half, 16), half)
     for s in range(nz):
-        wg_ref[mine, chunk_w * s : chunk_w * (s + 1)] = gbuf[c, s]
+        wg_ref[mine, chunk_w * s : chunk_w * (s + 1)] = gbuf[c, s].astype(jnp.float32) * grad_scale
     for s in range(nz):
         d_from(s).wait_recv()
-        wg_ref[theirs, chunk_w * s : chunk_w * (s + 1)] = gbuf[1 - c, s]
+        wg_ref[theirs, chunk_w * s : chunk_w * (s + 1)] = gbuf[1 - c, s].astype(jnp.float32) * grad_scale
 
     @pl.when(t < nt - 1)
     def _():
@@ -675,8 +679,7 @@
         ((chunks, KW, LANES), f32),
         ((KW, per_piece, 8, LANES), f32),
         ((KW, per_piece, span, LANES), f32),
-        ((head_width, chunk_w), f32),
-        ((nz, nf, half, chunk_w), f32),
+        ((nz, head_width, chunk_w), f32),
         ((nz, nf, half, chunk_w), bf16),
         ((nz, nf, half, chunk_w), bf16),
         ((nz, nf, half, chunk_w), bf16),
@@ -700,7 +703,7 @@
         functools.partial(block_kernel, nt, nf),
         out_shape=(
             jax.ShapeDtypeStruct((rows, head_width), bf16),
-            jax.ShapeDtypeStruct((shard, width), bf16),
+            jax.ShapeDtypeStruct((shard, width), f32),
             jax.ShapeDtypeStruct((KW, width // nf), f32),
         ),
         in_specs=[pl.BlockSpec(memory_space=pltpu.SMEM)] + [pl.BlockSpec(memory_space=pltpu.HBM)] * 6,
@@ -712,12 +715,7 @@
             collective_id=0, has_side_effects=True, vmem_limit_bytes=60 * 1024 * 1024
         ),
     )(utt_starts, queries[0], keys_values[0], inputs[0], cotangent[0], out_weight, conv_kernel)
-    grad_scale = 1.0 / math.sqrt(nf * queries.shape[0] * nt * rows)
-    return (
-        context_grad[None],
-        weight_grad.astype(jnp.float32) * grad_scale,
-        kernel_grad * grad_scale,
-    )
+    return (context_grad[None], weight_grad, kernel_grad)
 
 
 def fits(nt, nf, queries, keys_values, inputs, cotangent, out_weight, conv_kernel, utt_starts):

time: 63.6 us -> 61.5 us (0.967)
  local copies, waits for them, and re-layouts: 0.68 us -> 4.61 us
  other arithmetic: 3.67 us -> 0 us
  Pallas kernels: 58.4 us -> 56.1 us
    unnamed x3 -> x5, local copies, waits for them, and re-layouts: 0.68 us -> 4.61 us
    mul x2 -> x0, other arithmetic: 3.67 us -> none  [the longest x1 2.21 us: fused(): weight_grad.astype(jnp.float32) * grad_scale]
    pallas_call x1, Pallas kernels: 58.4 us -> 56.1 us  [fused(): pl.pallas_call(functools.partial(block_kernel, nt, nf), out_shape=(jax.Sh...]
where the time goes in v4:
time: 61.5 us; the launch traced here: 61.4 us
  Pallas kernels  56.1 us (91%)
  local copies, waits for them, and re-layouts  4.61 us (7%)
  between operations  0.64 us (1%)
    pallas_call x1, Pallas kernels, fused(): pl.pallas_call(functools.partial(block_kernel, nt, nf), out_shape=(jax.Sh...  56.1 us
    unnamed x5, local copies, waits for them, and re-layouts  4.61 us

profile of v4, /device:TPU:1, one launch (start us, length us, event | category | flops | bytes accessed | tf_op | source)
XLA Modules:
  0.0 61.4 jit_solution(4157494920932556848)
XLA Ops:
  0.6 56.1 %shard_map.94 = (bf16[128,768]{1,0:T(8,128)(2,1)}, f32[192,1536]{1,0:T(8,128)}, f32[32,384]{1,0:T(8,128)}) custom-call(s32[1,16]{1,0:T(1,128)} %starts_ref.1, bf16[128,768]{1,0:T(8,128)(2,1)} %bitcast.8, bf16[128,1536]{1,0:T(8,128)(2,1)} %bitcast.5, bf16[128,1536]{1,0:T(8,128)(2,1)} %bitcast.6, bf16[128,1536]{1,0:T(8,128)(2,1)} %bitcast.7, ...), custom_call_target="tpu_custom_call" | custom-call | tf_op jit(solution)/shard_map/pallas_call | solution.py:702
  56.8 1.6 %copy.13 = bf16[1,128,768]{2,1,0:T(8,128)(2,1)} copy(bf16[1,128,768]{2,1,0:T(8,128)(2,1)} %bitcast.9) | data formatting | bytes 393216
  58.4 0.0 copy-start
  58.4 2.4 %copy.14 = f32[192,1536]{1,0:T(8,128)} copy(f32[192,1536]{1,0:T(8,128)} %get-tuple-element.13) | data formatting | bytes 2359296
  60.7 0.0 copy-done
  60.8 0.6 %copy.15 = f32[32,384]{1,0:T(8,128)} copy(f32[32,384]{1,0:T(8,128)S(1)} %copy-done) | data formatting | bytes 98304
Async XLA Ops:
  58.4 2.4 %copy-start = (f32[32,384]{1,0:T(8,128)S(1)}, f32[32,384]{1,0:T(8,128)}, u32[]{:S(2)}) copy-start(f32[32,384]{1,0:T(8,128)} %get-tuple-element.14) | copy-start | bytes 147460

commit v5 on v4

--- a/solution.py
+++ b/solution.py
@@ -444,6 +444,10 @@
             gs[:, lead : lead + GROUP] = cot_rows(lead) * sig * (1.0 + conv * (1.0 - sig))
         if j >= 1:
             finish_a(j - 1)
+        if j >= 2:
+            finish_b(j - 2)
+        if j >= 3:
+            finish_c(j - 3)
         for lead in range(0, rows, GROUP):
             mid = slice(COT_PAD + lead, COT_PAD + lead + GROUP)
             back = tiles(cot_rows(COT_PAD + lead))
@@ -547,10 +551,6 @@
         for s in range(nf):
             asrc[j, s] = part[j, rows_of(s, 1 - c)].astype(jnp.bfloat16)
         a_copy(j).start()
-        if j >= 2:
-            finish_b(j - 2)
-        if j >= 3:
-            finish_c(j - 3)
 
     def kb_copy(i):
         return copy(kgsrc.at[other_f(i)], kgb.at[i], kbs.at[i], kbr.at[i], t, other_f(i))

time: 61.5 us -> 62.6 us (1.018)
  Pallas kernels: 56.1 us -> 57.2 us
    pallas_call x1, Pallas kernels: 56.1 us -> 57.2 us  [fused(): pl.pallas_call(functools.partial(block_kernel, nt, nf), out_shape=(jax.Sh...]
where the time goes in v5:
time: 62.6 us; the launch traced here: 62.4 us
  Pallas kernels  57.2 us (91%)
  local copies, waits for them, and re-layouts  4.61 us (7%)
  between operations  0.64 us (1%)
    pallas_call x1, Pallas kernels, fused(): pl.pallas_call(functools.partial(block_kernel, nt, nf), out_shape=(jax.Sh...  57.2 us
    unnamed x5, local copies, waits for them, and re-layouts  4.61 us

profile of v5, /device:TPU:1, one launch (start us, length us, event | category | flops | bytes accessed | tf_op | source)
XLA Modules:
  0.0 62.4 jit_solution(2694675326569984986)
XLA Ops:
  0.6 57.2 %shard_map.94 = (bf16[128,768]{1,0:T(8,128)(2,1)}, f32[192,1536]{1,0:T(8,128)}, f32[32,384]{1,0:T(8,128)}) custom-call(s32[1,16]{1,0:T(1,128)} %starts_ref.1, bf16[128,768]{1,0:T(8,128)(2,1)} %bitcast.8, bf16[128,1536]{1,0:T(8,128)(2,1)} %bitcast.5, bf16[128,1536]{1,0:T(8,128)(2,1)} %bitcast.6, bf16[128,1536]{1,0:T(8,128)(2,1)} %bitcast.7, ...), custom_call_target="tpu_custom_call" | custom-call | tf_op jit(solution)/shard_map/pallas_call | solution.py:702
  57.8 1.6 %copy.13 = bf16[1,128,768]{2,1,0:T(8,128)(2,1)} copy(bf16[1,128,768]{2,1,0:T(8,128)(2,1)} %bitcast.9) | data formatting | bytes 393216
  59.5 0.0 copy-start
  59.5 2.4 %copy.14 = f32[192,1536]{1,0:T(8,128)} copy(f32[192,1536]{1,0:T(8,128)} %get-tuple-element.13) | data formatting | bytes 2359296
  61.8 0.0 copy-done
  61.8 0.6 copy.15
Async XLA Ops:
  59.5 2.4 %copy-start = (f32[32,384]{1,0:T(8,128)S(1)}, f32[32,384]{1,0:T(8,128)}, u32[]{:S(2)}) copy-start(f32[32,384]{1,0:T(8,128)} %get-tuple-element.14) | copy-start | bytes 147460
